TPU v7x, 512 devices: a whole 4x4x16 slice. The times are simulated.
512 devices in a mesh: ctx: 64 (over z_hi, x, y), tp: 8 (over z_lo, core).
Axes of the slice: x: 4, y: 4, z: 16 (z_hi: 4, z_lo: 4; z = z_hi * 4 + z_lo), core: 2. Of those that a mesh axis runs over, the one named last changes fastest.
Arguments:
- tokens: bfloat16 [16384, 2688], P(('ctx', 'tp')), may hold values from -6 to 6
- result_grad: bfloat16 [16384, 2688], P(('ctx', 'tp')), may hold values from -6 to 6
- query_weight: bfloat16 [2688, 2048], P(None, 'tp'), may hold values from -0.125 to 0.125
- key_weight: bfloat16 [2688, 1024], P(None, 'tp'), may hold values from -0.125 to 0.125
- value_weight: bfloat16 [2688, 1024], P(None, 'tp'), may hold values from -0.125 to 0.125
- output_weight: bfloat16 [2048, 2688], P('tp'), may hold values from -0.5 to 0.5
- query_gain: float32 [128], replicated, may hold values from 0.5 to 1.5
- key_gain: float32 [128], replicated, may hold values from 0.5 to 1.5
Outputs:
- layer_output: bfloat16 [16384, 2688], P(('ctx', 'tp'))
- tokens_grad: bfloat16 [16384, 2688], P(('ctx', 'tp'))
All inputs are finite; a program needn't handle non-finite values.
Results may differ from a plain program's by a relative error of at most 0.012.
Values may be sent and summed in bfloat16 or wider, within the bound.
No kernel may reach another device: no remote copies, remote signals or barrier semaphores. Data moves between devices by JAX's collectives and lax.ppermute only.
A program may use at most 64 MiB of HBM per device.

v0:
```python
import jax
import jax.numpy as jnp
from jax import lax
from jax.sharding import PartitionSpec as P

WINDOW = 1024


norm_epsilon = 1e-06
score_scale = 168.0 ** (-0.5)
rope_theta = 10000.0


def from_behind(block, axis, distance):
    devices = range(lax.axis_size(axis))
    route = [(i - distance, i) for i in devices if i - distance in devices]
    return lax.ppermute(block, axis, route)


def rope_tables(positions, head_size):
    half_size = head_size // 2
    exponent = jnp.arange(half_size, dtype=jnp.float32) * (2.0 / head_size)
    frequency = jnp.power(jnp.float32(rope_theta), -exponent)
    angles = positions.astype(jnp.float32)[:, None] * frequency[None, :]
    return (jnp.cos(angles), jnp.sin(angles))


def norm_rope(raw_proj, scale_gain, cosines, sines):
    row_count = raw_proj.shape[0]
    head_size = scale_gain.shape[0]
    split_heads = raw_proj.reshape(row_count, -1, head_size)
    mean_square = jnp.mean(split_heads * split_heads, axis=-1, keepdims=True)
    normed = split_heads * lax.rsqrt(mean_square + norm_epsilon) * scale_gain
    half_size = head_size // 2
    low_half = normed[..., :half_size]
    high_half = normed[..., half_size:]
    cosine_b = cosines[:, None, :]
    sine_b = sines[:, None, :]
    return jnp.concatenate(
        [low_half * cosine_b - high_half * sine_b, high_half * cosine_b + low_half * sine_b],
        axis=-1,
    )


def attend(queries, keys_all, values_all, out_grad, query_first, key_first):
    query_count = queries.shape[0]
    key_count = keys_all.shape[0]
    scores = (
        jnp.einsum("qkgh,ckh->kgqc", queries, keys_all, preferred_element_type=jnp.float32)
        * score_scale
    )
    query_pos = query_first + jnp.arange(query_count, dtype=jnp.int32)
    key_pos = key_first + jnp.arange(key_count, dtype=jnp.int32)
    distance = query_pos[:, None] - key_pos[None, :]
    allowed = (distance >= 0) & (distance < WINDOW) & (key_pos[None, :] >= 0)
    weights_raw = jnp.where(allowed, jnp.exp(scores), jnp.float32(0.0))
    denominator = jnp.sum(weights_raw, axis=-1, keepdims=True)
    weights_soft = weights_raw / denominator
    weights_low = weights_soft.astype(jnp.bfloat16)
    attended_wide = jnp.einsum(
        "kgqc,ckh->qkgh", weights_low, values_all, preferred_element_type=jnp.float32
    )
    attended = lax.optimization_barrier(attended_wide.astype(jnp.bfloat16))
    row_dots = jnp.sum(out_grad.astype(jnp.float32) * attended.astype(jnp.float32), axis=-1)
    prob_grad = jnp.einsum(
        "qkgh,ckh->kgqc", out_grad, values_all, preferred_element_type=jnp.float32
    )
    centered = prob_grad - jnp.transpose(row_dots, (1, 2, 0))[..., None]
    score_grad = (weights_soft * centered * score_scale).astype(jnp.bfloat16)
    query_grad = jnp.einsum(
        "kgqc,ckh->qkgh", score_grad, keys_all, preferred_element_type=jnp.float32
    )
    key_grad = jnp.einsum("kgqc,qkgh->ckh", score_grad, queries, preferred_element_type=jnp.float32)
    value_grad = jnp.einsum(
        "kgqc,qkgh->ckh", weights_low, out_grad, preferred_element_type=jnp.float32
    )
    return (attended, query_grad, key_grad, value_grad)


def on_device(
    tokens, result_grad, query_weight, key_weight, value_weight, output_weight, query_gain, key_gain
):
    local_rows = tokens.shape[0]
    row_count = local_rows * lax.axis_size("tp")
    head_size = query_gain.shape[0]
    query_cols = query_weight.shape[1]
    kv_cols = key_weight.shape[1]
    kv_count = kv_cols // head_size
    per_kv = query_cols // kv_cols
    stacked = jnp.stack([tokens, result_grad])
    portion = lax.all_gather(stacked, "tp", axis=1, tiled=True)
    inputs_part = portion[0]
    gradients_part = portion[1]
    query_rows = jnp.dot(inputs_part, query_weight, preferred_element_type=jnp.float32)
    key_rows = jnp.dot(inputs_part, key_weight, preferred_element_type=jnp.float32)
    value_rows = jnp.dot(inputs_part, value_weight, preferred_element_type=jnp.float32)
    grad_rows = jnp.einsum(
        "nd,hd->nh", gradients_part, output_weight, preferred_element_type=jnp.float32
    )
    joined = jnp.concatenate([query_rows, key_rows, value_rows, grad_rows], axis=1)
    query_raw = joined[:, :query_cols]
    key_raw = joined[:, query_cols : query_cols + kv_cols]
    value_raw = joined[:, query_cols + kv_cols : query_cols + 2 * kv_cols]
    out_grad = (
        joined[:, query_cols + 2 * kv_cols :]
        .astype(jnp.bfloat16)
        .reshape(row_count, kv_count, per_kv, head_size)
    )
    row_first = lax.axis_index("ctx") * row_count
    positions = row_first + jnp.arange(row_count, dtype=jnp.int32)
    cosines, sines = rope_tables(positions, head_size)
    queries = (
        norm_rope(query_raw, query_gain, cosines, sines)
        .astype(jnp.bfloat16)
        .reshape(row_count, kv_count, per_kv, head_size)
    )
    keys_own = norm_rope(key_raw, key_gain, cosines, sines).astype(jnp.bfloat16)
    values_own = value_raw.astype(jnp.bfloat16).reshape(row_count, kv_count, head_size)
    tail_rows = min(row_count, WINDOW)
    reach = WINDOW // tail_rows
    own_tail = jnp.stack([keys_own, values_own])
    arrivals = []
    message = own_tail
    for stride in range(1, reach + 1):
        sender = own_tail
        distance = stride
        message = from_behind(sender, "ctx", distance)
        arrivals.append(message)
    halo_rows = jnp.concatenate(arrivals[::-1], axis=1)
    keys_all = jnp.concatenate([halo_rows[0], keys_own], axis=0)
    values_all = jnp.concatenate([halo_rows[1], values_own], axis=0)
    attended, query_grad, key_grad, value_grad = attend(
        queries, keys_all, values_all, out_grad, row_first, row_first - WINDOW
    )
    attended_flat = attended.reshape(row_count, query_cols)
    halo_grad = jnp.stack([key_grad[:WINDOW], value_grad[:WINDOW]])
    returned = jnp.zeros((2, tail_rows, kv_count, head_size), jnp.float32)
    for turn_index in range(reach):
        portion_stride = turn_index + 1
        sender = halo_grad[
            :, WINDOW - portion_stride * tail_rows : WINDOW - (portion_stride - 1) * tail_rows
        ]
        distance = -(turn_index + 1)
        arrived = from_behind(sender.astype(jnp.bfloat16), "ctx", distance).astype(sender.dtype)
        returned = returned + arrived
    keep_rows = row_count - tail_rows
    key_grad_own = key_grad[WINDOW:]
    value_grad_own = value_grad[WINDOW:]
    key_grad_own = jnp.concatenate([key_grad_own[:keep_rows], key_grad_own + returned[0]], axis=0)
    value_grad_own = jnp.concatenate(
        [value_grad_own[:keep_rows], value_grad_own + returned[1]], axis=0
    )

    def query_shape(raw_proj):
        return norm_rope(raw_proj, query_gain, cosines, sines)

    def key_shape(raw_proj):
        return norm_rope(raw_proj, key_gain, cosines, sines)

    query_back = jax.vjp(query_shape, query_raw)[1](query_grad.reshape(row_count, -1, head_size))[
        0
    ].astype(jnp.bfloat16)
    key_back = jax.vjp(key_shape, key_raw)[1](key_grad_own)[0].astype(jnp.bfloat16)
    value_back = value_grad_own.reshape(row_count, kv_cols).astype(jnp.bfloat16)
    out_part = jnp.dot(attended_flat, output_weight, preferred_element_type=jnp.float32)
    query_rows = query_back
    key_rows = key_back
    value_rows = value_back
    summed = jnp.einsum("nh,dh->nd", query_rows, query_weight, preferred_element_type=jnp.float32)
    summed = summed + jnp.einsum(
        "nh,dh->nd", key_rows, key_weight, preferred_element_type=jnp.float32
    )
    summed = summed + jnp.einsum(
        "nh,dh->nd", value_rows, value_weight, preferred_element_type=jnp.float32
    )
    out_sum, grad_sum = (
        lax.psum_scatter(
            out_part.astype(jnp.bfloat16), "tp", scatter_dimension=0, tiled=True
        ).astype(jnp.float32),
        lax.psum_scatter(summed.astype(jnp.bfloat16), "tp", scatter_dimension=0, tiled=True).astype(
            jnp.float32
        ),
    )
    layer_output = (tokens.astype(jnp.float32) + out_sum).astype(jnp.bfloat16)
    tokens_grad = (result_grad.astype(jnp.float32) + grad_sum).astype(jnp.bfloat16)
    return (layer_output, tokens_grad)


def solution(mesh):
    in_specs = (
        P(("ctx", "tp"), None),
        P(("ctx", "tp"), None),
        P(None, "tp"),
        P(None, "tp"),
        P(None, "tp"),
        P("tp", None),
        P(),
        P(),
    )
    out_specs = (P(("ctx", "tp"), None), P(("ctx", "tp"), None))
    return jax.shard_map(
        on_device, mesh=mesh, in_specs=in_specs, out_specs=out_specs, check_vma=False
    )
```

profile of v0, /device:TPU:6, one launch (start us, length us, event | category | flops | bytes accessed | tf_op | source)
XLA Modules:
  0.0 222.6 jit_solution(2841424224340872618)
XLA Ops:
  7.2 1.9 pad_maximum_fusion
  9.2 1.8 copy.30
  11.4 1.6 fusion.20
  13.0 48.1 %all-gather.2.cloned.1.call-done = bf16[2,256,2688]{2,1,0:T(8,128)(2,1)} async-done(((bf16[2,32,2688]{2,1,0:T(8,128)(2,1)}), bf16[2,256,2688]{2,1,0:T(8,128)(2,1)}) %all-gather.2.cloned.1.call-update) | async-done | bytes 2752528 | tf_op jit(solution)/shard_map/all_gather | solution.py:91
  61.1 2.2 multiply_reduce_fusion.2
  63.8 2.2 fusion.28
  66.0 3.4 %collective-permute-start.3 = (bf16[2,256,1,128]{1,3,2,0:T(8,128)(2,1)S(1)}, bf16[2,256,1,128]{1,3,2,0:T(8,128)(2,1)S(1)}, u32[]{:S(2)}, u32[]{:S(2)}) collective-permute-start(bf16[2,256,1,128]{1,3,2,0:T(8,128)(2,1)S(1)} %pad_maximum_fusion.1), channel_id=1, source_target_pairs={{0,8},{8,16},{16,24},{24,32},{32,40},{40,48},{48,56},{56,64},{64,7... | collective-permute-start | bytes 393224 | tf_op jit(solution)/shard_map/ppermute | solution.py:17
  69.4 4.6 %collective-permute-start.2 = (bf16[2,256,1,128]{1,3,2,0:T(8,128)(2,1)S(1)}, bf16[2,256,1,128]{1,3,2,0:T(8,128)(2,1)S(1)}, u32[]{:S(2)}, u32[]{:S(2)}) collective-permute-start(bf16[2,256,1,128]{1,3,2,0:T(8,128)(2,1)S(1)} %pad_maximum_fusion.1), channel_id=1, source_target_pairs={{0,16},{8,24},{16,32},{24,40},{32,48},{40,56},{48,64},{56,72},{64,... | collective-permute-start | bytes 393224 | tf_op jit(solution)/shard_map/ppermute | solution.py:17
  74.0 8.5 %collective-permute-start.1 = (bf16[2,256,1,128]{1,3,2,0:T(8,128)(2,1)S(1)}, bf16[2,256,1,128]{1,3,2,0:T(8,128)(2,1)S(1)}, u32[]{:S(2)}, u32[]{:S(2)}) collective-permute-start(bf16[2,256,1,128]{1,3,2,0:T(8,128)(2,1)S(1)} %pad_maximum_fusion.1), channel_id=1, source_target_pairs={{0,24},{8,32},{16,40},{24,48},{32,56},{40,64},{48,72},{56,80},{64,... | collective-permute-start | bytes 393224 | tf_op jit(solution)/shard_map/ppermute | solution.py:17
  82.5 3.4 %collective-permute-start = (bf16[2,256,1,128]{1,3,2,0:T(8,128)(2,1)S(1)}, bf16[2,256,1,128]{1,3,2,0:T(8,128)(2,1)S(1)}, u32[]{:S(2)}, u32[]{:S(2)}) collective-permute-start(bf16[2,256,1,128]{1,3,2,0:T(8,128)(2,1)S(1)} %pad_maximum_fusion.1), channel_id=1, source_target_pairs={{0,32},{8,40},{16,48},{24,56},{32,64},{40,72},{48,80},{56,88},{64,... | collective-permute-start | bytes 393224 | tf_op jit(solution)/shard_map/ppermute | solution.py:17
  87.3 2.1 collective-permute-done
  93.2 0.9 fusion.72
  94.1 1.7 convolution_convert_fusion
  95.8 2.9 %collective-permute-start.4 = (bf16[2,256,1,128]{1,3,2,0:T(8,128)(2,1)}, bf16[2,256,1,128]{1,3,2,0:T(8,128)(2,1)S(1)}, u32[]{:S(2)}, u32[]{:S(2)}) collective-permute-start(bf16[2,256,1,128]{1,3,2,0:T(8,128)(2,1)} %get-tuple-element.2), channel_id=1, source_target_pairs={{8,0},{16,8},{24,16},{32,24},{40,32},{48,40},{56,48},{64,56},{72,6... | collective-permute-start | bytes 393224 | tf_op jit(solution)/shard_map/ppermute | solution.py:17
  98.7 1.9 collective-permute-start.7
  100.6 2.1 collective-permute-start.6
  102.8 3.3 %collective-permute-start.5 = (bf16[2,256,1,128]{1,3,2,0:T(8,128)(2,1)}, bf16[2,256,1,128]{1,3,2,0:T(8,128)(2,1)S(1)}, u32[]{:S(2)}, u32[]{:S(2)}) collective-permute-start(bf16[2,256,1,128]{1,3,2,0:T(8,128)(2,1)} %get-tuple-element.5), channel_id=1, source_target_pairs={{16,0},{24,8},{32,16},{40,24},{48,32},{56,40},{64,48},{72,56},{80,... | collective-permute-start | bytes 393224 | tf_op jit(solution)/shard_map/ppermute | solution.py:17
  108.3 4.6 %collective-permute-done.7 = bf16[2,256,1,128]{1,3,2,0:T(8,128)(2,1)S(1)} collective-permute-done((bf16[2,256,1,128]{1,3,2,0:T(8,128)(2,1)}, bf16[2,256,1,128]{1,3,2,0:T(8,128)(2,1)S(1)}, u32[]{:S(2)}, u32[]{:S(2)}) %collective-permute-start.7) | collective-permute-done | bytes 131104 | tf_op jit(solution)/shard_map/ppermute | solution.py:17
  113.0 0.9 fusion.40
  115.5 2.5 %fusion = bf16[256,2688]{1,0:T(8,128)(2,1)} fusion(f32[256,2688]{1,0:T(8,128)S(1)} %convolution_add_fusion.1, bf16[2688,128]{1,0:T(8,128)(2,1)S(1)} %copy-done.6, f32[2,256,1,128]{1,3,2,0:T(8,128)S(1)} %convert_add_fusion, f32[1280,1,128]{0,2,1:T(8,128)} %copy-done.2), kind=kOutput, calls=%fused_computation.2 | convolution fusion | flops 177602560 | bytes 5079040 | tf_op jit(solution)/shard_map/nh,dh->nd/dot_general | solution.py:173
  118.1 49.2 %reduce-scatter.3.cloned.1.call-done = bf16[32,2688]{1,0:T(8,128)(2,1)} async-done(((bf16[256,2688]{1,0:T(8,128)(2,1)}), bf16[32,2688]{1,0:T(8,128)(2,1)}) %reduce-scatter.3.cloned.1.call-update) | async-done | bytes 172048 | tf_op jit(solution)/shard_map/reduce_scatter | solution.py:177
  167.3 1.6 add_convert_fusion.1
  168.9 45.5 %reduce-scatter.5.cloned.1.call-done = bf16[32,2688]{1,0:T(8,128)(2,1)} async-done(((bf16[256,2688]{1,0:T(8,128)(2,1)}), bf16[32,2688]{1,0:T(8,128)(2,1)}) %reduce-scatter.5.cloned.1.call-update) | async-done | bytes 172048 | tf_op jit(solution)/shard_map/reduce_scatter | solution.py:180
  214.5 1.6 add_convert_fusion
  (88 shorter events, 9.8 us)
Async XLA Ops:
  7.2 79.5 %copy-start = (bf16[256,2688]{1,0:T(8,128)(2,1)S(1)}, bf16[256,2688]{1,0:T(8,128)(2,1)}, u32[]{:S(2)}) copy-start(bf16[256,2688]{1,0:T(8,128)(2,1)} %param.13) | copy-start | bytes 4128772
  7.2 53.9 %all-gather.2.cloned.1.call-start = ((), (), s32[]{:S(2)}) async-start(), calls=%async_computation.2 | async-start | bytes 3096576 | tf_op jit(solution)/shard_map/all_gather | solution.py:91
  9.1 158.1 %reduce-scatter.3.cloned.1.call-start = ((), (), s32[]{:S(2)}) async-start(), calls=%async_computation.3 | async-start | bytes 1548288 | tf_op jit(solution)/shard_map/reduce_scatter | solution.py:177
  11.0 52.4 %copy-start.12 = (f32[64]{0:T(128)}, f32[64]{0:T(128)S(1)}, u32[]{:S(2)}) copy-start(f32[64]{0:T(128)S(1)} %negate_power_fusion) | copy-start | bytes 772
  11.1 52.3 %copy-start.10 = (f32[128]{0:T(128)S(1)}, f32[128]{0:T(128)}, u32[]{:S(2)}) copy-start(f32[128]{0:T(128)} %param.15) | copy-start | bytes 1540
  61.1 2.7 %copy-start.5 = (bf16[2688,128]{1,0:T(8,128)(2,1)S(1)}, bf16[2688,128]{1,0:T(8,128)(2,1)}, u32[]{:S(2)}) copy-start(bf16[2688,128]{1,0:T(8,128)(2,1)} %param.12) | copy-start | bytes 2064388
  63.3 2.7 %copy-start.15 = (f32[256]{0:T(256)}, f32[256]{0:T(256)S(1)}, u32[]{:S(2)}) copy-start(f32[256]{0:T(256)S(1)} %get-tuple-element.18) | copy-start | bytes 3076
  63.3 22.6 %copy-start.17 = (bf16[2,256,2688]{2,1,0:T(8,128)(2,1)S(1)}, bf16[2,256,2688]{2,1,0:T(8,128)(2,1)}, u32[]{:S(2)}) copy-start(bf16[2,256,2688]{2,1,0:T(8,128)(2,1)} %all-gather.2.cloned.1.call-done) | copy-start | bytes 8257540
  66.0 23.5 %collective-permute-start.3 = (bf16[2,256,1,128]{1,3,2,0:T(8,128)(2,1)S(1)}, bf16[2,256,1,128]{1,3,2,0:T(8,128)(2,1)S(1)}, u32[]{:S(2)}, u32[]{:S(2)}) collective-permute-start(bf16[2,256,1,128]{1,3,2,0:T(8,128)(2,1)S(1)} %pad_maximum_fusion.1), channel_id=1, source_target_pairs={{0,8},{8,16},{16,24},{24,32},{32,40},{40,48},{48,56},{56,64},{64,7... | collective-permute-start | bytes 393224 | tf_op jit(solution)/shard_map/ppermute | solution.py:17
  69.4 20.1 %collective-permute-start.2 = (bf16[2,256,1,128]{1,3,2,0:T(8,128)(2,1)S(1)}, bf16[2,256,1,128]{1,3,2,0:T(8,128)(2,1)S(1)}, u32[]{:S(2)}, u32[]{:S(2)}) collective-permute-start(bf16[2,256,1,128]{1,3,2,0:T(8,128)(2,1)S(1)} %pad_maximum_fusion.1), channel_id=1, source_target_pairs={{0,16},{8,24},{16,32},{24,40},{32,48},{40,56},{48,64},{56,72},{64,... | collective-permute-start | bytes 393224 | tf_op jit(solution)/shard_map/ppermute | solution.py:17
  74.0 15.4 %collective-permute-start.1 = (bf16[2,256,1,128]{1,3,2,0:T(8,128)(2,1)S(1)}, bf16[2,256,1,128]{1,3,2,0:T(8,128)(2,1)S(1)}, u32[]{:S(2)}, u32[]{:S(2)}) collective-permute-start(bf16[2,256,1,128]{1,3,2,0:T(8,128)(2,1)S(1)} %pad_maximum_fusion.1), channel_id=1, source_target_pairs={{0,24},{8,32},{16,40},{24,48},{32,56},{40,64},{48,72},{56,80},{64,... | collective-permute-start | bytes 393224 | tf_op jit(solution)/shard_map/ppermute | solution.py:17
  82.5 6.9 %collective-permute-start = (bf16[2,256,1,128]{1,3,2,0:T(8,128)(2,1)S(1)}, bf16[2,256,1,128]{1,3,2,0:T(8,128)(2,1)S(1)}, u32[]{:S(2)}, u32[]{:S(2)}) collective-permute-start(bf16[2,256,1,128]{1,3,2,0:T(8,128)(2,1)S(1)} %pad_maximum_fusion.1), channel_id=1, source_target_pairs={{0,32},{8,40},{16,48},{24,56},{32,64},{40,72},{48,80},{56,88},{64,... | collective-permute-start | bytes 393224 | tf_op jit(solution)/shard_map/ppermute | solution.py:17
  95.7 11.9 %copy-start.1 = (bf16[2688,256]{1,0:T(8,128)(2,1)S(1)}, bf16[2688,256]{1,0:T(8,128)(2,1)}, u32[]{:S(2)}) copy-start(bf16[2688,256]{1,0:T(8,128)(2,1)} %param.10) | copy-start | bytes 4128772
  95.8 118.7 %reduce-scatter.5.cloned.1.call-start = ((), (), s32[]{:S(2)}) async-start(), calls=%async_computation.4 | async-start | bytes 1548288 | tf_op jit(solution)/shard_map/reduce_scatter | solution.py:180
  95.8 12.5 %collective-permute-start.4 = (bf16[2,256,1,128]{1,3,2,0:T(8,128)(2,1)}, bf16[2,256,1,128]{1,3,2,0:T(8,128)(2,1)S(1)}, u32[]{:S(2)}, u32[]{:S(2)}) collective-permute-start(bf16[2,256,1,128]{1,3,2,0:T(8,128)(2,1)} %get-tuple-element.2), channel_id=1, source_target_pairs={{8,0},{16,8},{24,16},{32,24},{40,32},{48,40},{56,48},{64,56},{72,6... | collective-permute-start | bytes 393224 | tf_op jit(solution)/shard_map/ppermute | solution.py:17
  98.7 14.2 %collective-permute-start.7 = (bf16[2,256,1,128]{1,3,2,0:T(8,128)(2,1)}, bf16[2,256,1,128]{1,3,2,0:T(8,128)(2,1)S(1)}, u32[]{:S(2)}, u32[]{:S(2)}) collective-permute-start(bf16[2,256,1,128]{1,3,2,0:T(8,128)(2,1)} %get-tuple-element.3), channel_id=1, source_target_pairs={{32,0},{40,8},{48,16},{56,24},{64,32},{72,40},{80,48},{88,56},{96,... | collective-permute-start | bytes 393224 | tf_op jit(solution)/shard_map/ppermute | solution.py:17
  100.6 12.3 %collective-permute-start.6 = (bf16[2,256,1,128]{1,3,2,0:T(8,128)(2,1)}, bf16[2,256,1,128]{1,3,2,0:T(8,128)(2,1)S(1)}, u32[]{:S(2)}, u32[]{:S(2)}) collective-permute-start(bf16[2,256,1,128]{1,3,2,0:T(8,128)(2,1)} %get-tuple-element.4), channel_id=1, source_target_pairs={{24,0},{32,8},{40,16},{48,24},{56,32},{64,40},{72,48},{80,56},{88,... | collective-permute-start | bytes 393224 | tf_op jit(solution)/shard_map/ppermute | solution.py:17
  102.8 10.2 %collective-permute-start.5 = (bf16[2,256,1,128]{1,3,2,0:T(8,128)(2,1)}, bf16[2,256,1,128]{1,3,2,0:T(8,128)(2,1)S(1)}, u32[]{:S(2)}, u32[]{:S(2)}) collective-permute-start(bf16[2,256,1,128]{1,3,2,0:T(8,128)(2,1)} %get-tuple-element.5), channel_id=1, source_target_pairs={{16,0},{24,8},{32,16},{40,24},{48,32},{56,40},{64,48},{72,56},{80,... | collective-permute-start | bytes 393224 | tf_op jit(solution)/shard_map/ppermute | solution.py:17
  107.7 6.3 %copy-start.13 = (f32[64]{0:T(128)S(1)}, f32[64]{0:T(128)}, u32[]{:S(2)}) copy-start(f32[64]{0:T(128)} %copy-done.12) | copy-start | bytes 772
  108.3 6.0 %copy-start.11 = (f32[128]{0:T(128)S(1)}, f32[128]{0:T(128)}, u32[]{:S(2)}) copy-start(f32[128]{0:T(128)} %param.15) | copy-start | bytes 1540
  108.3 6.1 %copy-start.16 = (f32[256]{0:T(256)S(1)}, f32[256]{0:T(256)}, u32[]{:S(2)}) copy-start(f32[256]{0:T(256)} %copy-done.15) | copy-start | bytes 3076
  108.3 6.1 %copy-start.4 = (bf16[2688,128]{1,0:T(8,128)(2,1)S(1)}, bf16[2688,128]{1,0:T(8,128)(2,1)}, u32[]{:S(2)}) copy-start(bf16[2688,128]{1,0:T(8,128)(2,1)} %param.11) | copy-start | bytes 2064388
  118.1 49.2 %copy-start.7 = (bf16[32,2688]{1,0:T(8,128)(2,1)S(1)}, bf16[32,2688]{1,0:T(8,128)(2,1)}, u32[]{:S(2)}) copy-start(bf16[32,2688]{1,0:T(8,128)(2,1)} %param.8) | copy-start | bytes 516100
  118.1 96.4 %copy-start.8 = (bf16[32,2688]{1,0:T(8,128)(2,1)S(1)}, bf16[32,2688]{1,0:T(8,128)(2,1)}, u32[]{:S(2)}) copy-start(bf16[32,2688]{1,0:T(8,128)(2,1)} %param.9) | copy-start | bytes 516100
  (5 other events, 7.0 us)
Sparse Core Ops, SparseCore 0:
  10.1 50.9 all-gather.1
  95.9 71.3 reduce-scatter.2
  170.4 44.0 reduce-scatter.4
where the time goes:
time: 223 us
  waiting for transfers between devices  150 us (67%)
  starting transfers between devices  30.2 us (14%)
  between operations  14.3 us (6%)
  matrix products  14.1 us (6%)
  other arithmetic  11 us (5%)
  local copies, waits for them, and re-layouts  3.38 us (2%)
    reduce_scatter x1, waiting for transfers between devices, on_device(): lax.psum_scatter(out_part.astype(jnp.bfloat16), 'tp', scatter_dimension=0...  49.2 us
    all_gather x1, waiting for transfers between devices, on_device(): portion = lax.all_gather(stacked, 'tp', axis=1, tiled=True)  48.1 us
    reduce_scatter x1, waiting for transfers between devices, on_device(): lax.psum_scatter(summed.astype(jnp.bfloat16), 'tp', scatter_dimension=0,...  45.5 us
    ppermute x8, starting transfers between devices, from_behind(): return lax.ppermute(block, axis, route)  30.1 us
    ppermute x8, waiting for transfers between devices, from_behind(): return lax.ppermute(block, axis, route)  6.7 us
  transfers between devices with their start and end apart: 11, of which 5 were waited for; matrix products, arithmetic and copies ran while one was open for 6% of the time, Pallas kernels for 0%

commit v1 on v0

v1 whole, which is shorter than its diff:
```python
import jax
import jax.numpy as jnp
from jax import lax
from jax.sharding import Mesh, PartitionSpec as P

WINDOW = 1024
ALL = ("zh", "x", "y", "zl", "c")
TP = ("zl", "c")

norm_epsilon = 1e-06
score_scale = 168.0 ** (-0.5)
rope_theta = 10000.0
f32 = jnp.float32
bf16 = jnp.bfloat16


def swap_cores(block):
    return lax.ppermute(block, "c", [(0, 1), (1, 0)])


def shift_rows(block, step):
    count = lax.axis_size(("zh", "x"))
    route = [(i, i + step) for i in range(count) if 0 <= i + step < count]
    return lax.ppermute(block, ("zh", "x"), route)


def rope_tables(positions, head_size):
    half_size = head_size // 2
    exponent = jnp.arange(half_size, dtype=f32) * (2.0 / head_size)
    frequency = jnp.power(f32(rope_theta), -exponent)
    angles = positions.astype(f32)[:, None] * frequency[None, :]
    return (jnp.cos(angles), jnp.sin(angles))


def norm_rope(raw_proj, scale_gain, cosines, sines):
    row_count = raw_proj.shape[0]
    head_size = scale_gain.shape[0]
    split_heads = raw_proj.reshape(row_count, -1, head_size)
    mean_square = jnp.mean(split_heads * split_heads, axis=-1, keepdims=True)
    normed = split_heads * lax.rsqrt(mean_square + norm_epsilon) * scale_gain
    half_size = head_size // 2
    low_half = normed[..., :half_size]
    high_half = normed[..., half_size:]
    cosine_b = cosines[:, None, :]
    sine_b = sines[:, None, :]
    return jnp.concatenate(
        [low_half * cosine_b - high_half * sine_b, high_half * cosine_b + low_half * sine_b],
        axis=-1,
    )


def attend(queries, keys_all, values_all, out_grad, query_pos, key_pos):
    scores = jnp.einsum("qgh,ch->gqc", queries, keys_all, preferred_element_type=f32) * score_scale
    distance = query_pos[:, None] - key_pos[None, :]
    allowed = (distance >= 0) & (distance < WINDOW) & (key_pos[None, :] >= 0)
    weights_raw = jnp.where(allowed, jnp.exp(scores), f32(0.0))
    denominator = jnp.sum(weights_raw, axis=-1, keepdims=True)
    weights_soft = weights_raw / denominator
    weights_low = weights_soft.astype(bf16)
    attended = lax.optimization_barrier(
        jnp.einsum("gqc,ch->qgh", weights_low, values_all, preferred_element_type=f32).astype(bf16)
    )
    row_dots = jnp.sum(out_grad.astype(f32) * attended.astype(f32), axis=-1)
    prob_grad = jnp.einsum("qgh,ch->gqc", out_grad, values_all, preferred_element_type=f32)
    centered = prob_grad - jnp.transpose(row_dots, (1, 0))[..., None]
    score_grad = (weights_soft * centered * score_scale).astype(bf16)
    query_grad = jnp.einsum("gqc,ch->qgh", score_grad, keys_all, preferred_element_type=f32)
    key_grad = jnp.einsum("gqc,qgh->ch", score_grad, queries, preferred_element_type=f32)
    value_grad = jnp.einsum("gqc,qgh->ch", weights_low, out_grad, preferred_element_type=f32)
    return (attended, query_grad, key_grad, value_grad)


def on_device(
    tokens, result_grad, query_weight, key_weight, value_weight, output_weight, query_gain, key_gain
):
    local_rows, width = tokens.shape
    n_zl = lax.axis_size("zl")
    n_y = lax.axis_size("y")
    row_count = local_rows * n_zl * lax.axis_size("c")
    head_size = query_gain.shape[0]
    core = lax.axis_index("c")
    y = lax.axis_index("y")
    query_cols = query_weight.shape[1]
    kv_cols = key_weight.shape[1]

    def order_rows(mine, other):
        cols = mine.shape[-1]
        first = jnp.where(core == 0, mine, other).reshape(n_zl, 1, local_rows, cols)
        second = jnp.where(core == 0, other, mine).reshape(n_zl, 1, local_rows, cols)
        return jnp.concatenate([first, second], axis=1).reshape(row_count, cols)

    gradients_part = lax.all_gather(result_grad, TP, axis=0, tiled=True)
    mine = lax.all_to_all(jnp.tile(tokens, (n_zl, 1)), "zl", 0, 0, tiled=True)
    other = swap_cores(mine)
    both = jnp.concatenate([mine, other], axis=0)

    def project(weight):
        rows = jnp.dot(both, weight, preferred_element_type=f32)
        half = rows.shape[0] // 2
        return order_rows(rows[:half], rows[half:])

    key_raw = project(key_weight)
    values_own = project(value_weight).astype(bf16)
    block = lax.axis_index(("zh", "x")) * n_y + y
    row_first = block * row_count
    positions = row_first + jnp.arange(row_count, dtype=jnp.int32)
    cosines, sines = rope_tables(positions, head_size)
    keys_own = norm_rope(key_raw, key_gain, cosines, sines).astype(bf16).reshape(row_count, head_size)
    own_kv = jnp.concatenate([keys_own, values_own], axis=1)
    above_kv = shift_rows(own_kv, 1)
    query_raw = project(query_weight)
    queries = (
        norm_rope(query_raw, query_gain, cosines, sines).astype(bf16).reshape(row_count, -1, head_size)
    )
    targets = jnp.arange(n_y, dtype=jnp.int32)
    outgoing = jnp.where((targets > y)[:, None, None], own_kv[None], above_kv[None])
    halo_kv = lax.all_to_all(outgoing, "y", 0, 0, tiled=True).reshape(n_y * row_count, 2 * head_size)
    base = lax.axis_index(("zh", "x")) * n_y * row_count
    halo_pos = (
        base
        + jnp.arange(n_y * row_count, dtype=jnp.int32)
        - jnp.where(jnp.repeat(targets, row_count) >= y, WINDOW, 0)
    )
    key_pos = jnp.concatenate([halo_pos, positions])
    all_kv = jnp.concatenate([halo_kv, own_kv], axis=0)

    out_grad = (
        jnp.einsum("nd,hd->nh", gradients_part, output_weight, preferred_element_type=f32)
        .astype(bf16)
        .reshape(row_count, -1, head_size)
    )
    attended, query_grad, key_grad, value_grad = attend(
        queries, all_kv[:, :head_size], all_kv[:, head_size:], out_grad, positions, key_pos
    )
    attended_flat = attended.reshape(row_count, query_cols)
    out_part = jnp.dot(attended_flat, output_weight, preferred_element_type=f32).astype(bf16)
    out_sum = lax.psum_scatter(out_part, TP, scatter_dimension=0, tiled=True).astype(f32)

    kv_grad = jnp.concatenate([key_grad, value_grad], axis=1)
    halo_grad = kv_grad[: n_y * row_count].astype(bf16).reshape(n_y, row_count, 2 * head_size)
    back = lax.all_to_all(halo_grad, "y", 0, 0, tiled=True).astype(f32)
    later = (targets > y)[:, None, None]
    back_own = jnp.sum(jnp.where(later, back, 0.0), axis=0)
    back_above = jnp.sum(jnp.where(later, 0.0, back), axis=0).astype(bf16)
    from_below = shift_rows(back_above, -1).astype(f32)

    def query_shape(raw_proj):
        return norm_rope(raw_proj, query_gain, cosines, sines)

    def key_shape(raw_proj):
        return norm_rope(raw_proj, key_gain, cosines, sines)

    query_back = jax.vjp(query_shape, query_raw)[1](query_grad)[0].astype(bf16)
    kv_own = kv_grad[n_y * row_count :] + back_own + from_below
    key_back = jax.vjp(key_shape, key_raw)[1](kv_own[:, None, :head_size])[0].astype(bf16)
    value_back = kv_own[:, head_size:].astype(bf16)

    def back_rows(which):
        def pick(array):
            split = array.reshape(n_zl, 2, local_rows, array.shape[-1])
            return lax.dynamic_index_in_dim(split, which, 1, keepdims=False).reshape(
                n_zl * local_rows, array.shape[-1]
            )

        dot = lambda a, w: jnp.einsum("nh,dh->nd", pick(a), w, preferred_element_type=f32)
        return (
            dot(query_back, query_weight) + dot(key_back, key_weight) + dot(value_back, value_weight)
        )

    given = swap_cores(back_rows(1 - core).astype(bf16))
    pair = (back_rows(core) + given.astype(f32)).astype(bf16)
    pieces = lax.all_to_all(pair, "zl", 0, 0, tiled=True).reshape(n_zl, local_rows, width)
    grad_sum = jnp.sum(pieces.astype(f32), axis=0)
    layer_output = (tokens.astype(f32) + out_sum).astype(bf16)
    tokens_grad = (result_grad.astype(f32) + grad_sum).astype(bf16)
    return (layer_output, tokens_grad)


def solution(mesh):
    fine = Mesh(mesh.devices.reshape(4, 4, 4, 4, 2), ALL)
    in_specs = (
        P(ALL, None),
        P(ALL, None),
        P(None, TP),
        P(None, TP),
        P(None, TP),
        P(TP, None),
        P(),
        P(),
    )
    out_specs = (P(ALL, None), P(ALL, None))
    return jax.shard_map(
        on_device, mesh=fine, in_specs=in_specs, out_specs=out_specs, check_vma=False
    )
```

time: 223 us -> 169 us (0.76)
  the two profiles are of different devices: /device:TPU:6 before, /device:TPU:47 now
where the time goes in v1:
time: 169 us
  waiting for transfers between devices  69.9 us (41%)
  starting transfers between devices  46.6 us (28%)
  matrix products  18.7 us (11%)
  between operations  14.6 us (9%)
  other arithmetic  13.9 us (8%)
  local copies, waits for them, and re-layouts  4.8 us (3%)
    reduce_scatter x1, waiting for transfers between devices, on_device(): lax.psum_scatter(out_part, TP, scatter_dimension=0, tiled=True).astype(f32)  28.7 us
    ppermute x2, waiting for transfers between devices, shift_rows(): return lax.ppermute(block, ('zh', 'x'), route)  17.6 us
    all_to_all x1, waiting for transfers between devices, on_device(): mine = lax.all_to_all(jnp.tile(tokens, (n_zl, 1)), 'zl', 0, 0, tiled=True)  13.2 us
    ppermute x2, starting transfers between devices, shift_rows(): return lax.ppermute(block, ('zh', 'x'), route)  10.8 us
    ppermute x2, starting transfers between devices, swap_cores(): return lax.ppermute(block, 'c', [(0, 1), (1, 0)])  10.7 us
    all_to_all x1, starting transfers between devices, on_device(): lax.all_to_all(pair, 'zl', 0, 0, tiled=True)  9.1 us
    all_to_all x1, waiting for transfers between devices, on_device(): lax.all_to_all(outgoing, 'y', 0, 0, tiled=True)  5.48 us
    all_to_all x1, starting transfers between devices, on_device(): mine = lax.all_to_all(jnp.tile(tokens, (n_zl, 1)), 'zl', 0, 0, tiled=True)  5.44 us
  transfers between devices with their start and end apart: 10, of which 7 were waited for; matrix products, arithmetic and copies ran while one was open for 15% of the time, Pallas kernels for 0%

profile of v1, /device:TPU:47, one launch (start us, length us, event | category | flops | bytes accessed | tf_op | source)
XLA Modules:
  0.0 168.5 jit_solution(8044469499146843883)
XLA Ops:
  7.2 2.0 %tile.2 = bf16[4,32,2688]{2,1,0:T(8,128)(2,1)} broadcast(bf16[32,2688]{1,0:T(8,128)(2,1)} %param.8), dimensions={1,2} | broadcast | bytes 860160 | tf_op jit(solution)/shard_map/tile | solution.py:93
  9.2 5.4 %all-to-all-start = ((bf16[4,32,2688]{2,1,0:T(8,128)(2,1)}), bf16[4,32,2688]{2,1,0:T(8,128)(2,1)S(1)}, u32[]{:S(2)}, u32[]{:S(2)}) async-start(bf16[4,32,2688]{2,1,0:T(8,128)(2,1)} %tile.2), calls=%async_computation | async-start | bytes 1376256 | tf_op jit(solution)/shard_map/all_to_all | solution.py:93
  15.5 13.2 %all-to-all-done = bf16[4,32,2688]{2,1,0:T(8,128)(2,1)S(1)} async-done(((bf16[4,32,2688]{2,1,0:T(8,128)(2,1)}), bf16[4,32,2688]{2,1,0:T(8,128)(2,1)S(1)}, u32[]{:S(2)}, u32[]{:S(2)}) %all-to-all-start) | async-done | bytes 688160 | tf_op jit(solution)/shard_map/all_to_all | solution.py:93
  28.7 3.8 %collective-permute-start = (bf16[128,2688]{1,0:T(8,128)(2,1)S(1)}, bf16[128,2688]{1,0:T(8,128)(2,1)S(1)}, u32[]{:S(2)}, u32[]{:S(2)}) collective-permute-start(bf16[128,2688]{1,0:T(8,128)(2,1)S(1)} %bitcast.103), channel_id=1, source_target_pairs={{0,1},{1,0},{2,3},{3,2},{4,5},{5,4},{6,7},{7,6},{8,9},{9,8},{10,11... | collective-permute-start | bytes 2064392 | tf_op jit(solution)/shard_map/ppermute | solution.py:18
  33.0 1.6 fusion.13
  36.7 1.8 %fusion.21 = bf16[256,128]{1,0:T(8,128)(2,1)S(1)} fusion(bf16[2688,128]{1,0:T(8,128)(2,1)S(1)} %copy-done.6, bf16[128,2688]{1,0:T(8,128)(2,1)} %copy-done.19, bf16[128,2688]{1,0:T(8,128)(2,1)S(1)} %bitcast.105), kind=kOutput, calls=%fused_computation.43 | convolution fusion | flops 178913280 | bytes 2129920 | tf_op jit(solution)/shard_map/dot_general | solution.py:98
  38.6 8.7 %collective-permute-start.1 = (bf16[256,256]{1,0:T(8,128)(2,1)S(1)}, bf16[256,256]{1,0:T(8,128)(2,1)}, u32[]{:S(2)}, u32[]{:S(2)}) collective-permute-start(bf16[256,256]{1,0:T(8,128)(2,1)S(1)} %pad_maximum_fusion.7), channel_id=1, source_target_pairs={{0,32},{32,64},{64,96},{96,128},{128,160},{160,192},{192,224},{224... | collective-permute-start | bytes 393224 | tf_op jit(solution)/shard_map/ppermute | solution.py:24
  48.6 5.4 %collective-permute-done.1 = bf16[256,256]{1,0:T(8,128)(2,1)} collective-permute-done((bf16[256,256]{1,0:T(8,128)(2,1)S(1)}, bf16[256,256]{1,0:T(8,128)(2,1)}, u32[]{:S(2)}, u32[]{:S(2)}) %collective-permute-start.1) | collective-permute-done | bytes 131104 | tf_op jit(solution)/shard_map/ppermute | solution.py:24
  54.0 1.8 %broadcast_select_fusion = bf16[4,256,256]{2,1,0:T(8,128)(2,1)} fusion(pred[4]{0:T(512)(128)(4,1)S(1)} %iota_compare_fusion.1, bf16[256,256]{1,0:T(8,128)(2,1)} %collective-permute-done.1, bf16[256,256]{1,0:T(8,128)(2,1)S(1)} %pad_maximum_fusion.7), kind=kLoop, calls=%fused_computation.41 | loop fusion | flops 262144 | bytes 786436 | tf_op jit(solution)/shard_map/jit(_where)/select_n | solution.py:116
  55.8 5.3 %all-to-all-start.1 = ((bf16[4,256,256]{2,1,0:T(8,128)(2,1)}), bf16[4,256,256]{2,1,0:T(8,128)(2,1)S(1)}, u32[]{:S(2)}, u32[]{:S(2)}) async-start(bf16[4,256,256]{2,1,0:T(8,128)(2,1)} %broadcast_select_fusion), calls=%async_computation.1 | async-start | bytes 1048576 | tf_op jit(solution)/shard_map/all_to_all | solution.py:117
  61.5 5.5 %all-to-all-done.1 = bf16[4,256,256]{2,1,0:T(8,128)(2,1)S(1)} async-done(((bf16[4,256,256]{2,1,0:T(8,128)(2,1)}), bf16[4,256,256]{2,1,0:T(8,128)(2,1)S(1)}, u32[]{:S(2)}, u32[]{:S(2)}) %all-to-all-start.1) | async-done | bytes 524320 | tf_op jit(solution)/shard_map/all_to_all | solution.py:117
  67.1 3.4 %fusion.11 = f32[2,256,1280]{1,2,0:T(8,128)} fusion(pred[256,1280]{0,1:T(8,128)(4,1)} %fusion.13, bf16[1280,256]{1,0:T(8,128)(2,1)S(1)} %maximum_maximum_fusion, bf16[256,2,64]{2,0,1:T(8,128)(2,1)S(1)} %get-tuple-element.7, bf16[256,2,64]{2,0,1:T(8,128)(2,1)S(1)} %get-tuple-element.6), kind=kOutput, calls=%fused_computation.27 | convolution fusion | flops 170002176 | bytes 3538944 | tf_op jit(solution)/shard_map/div | solution.py:58
  70.5 2.1 %fusion.14 = bf16[256,2,128]{0,2,1:T(8,128)(2,1)S(1)} fusion(f32[2,256,1280]{1,2,0:T(8,128)} %fusion.11, bf16[1280,256]{1,0:T(8,128)(2,1)S(1)} %maximum_maximum_fusion), kind=kOutput, calls=%fused_computation.33 | convolution fusion | flops 168493056 | bytes 3080192 | tf_op jit(solution)/shard_map/gqc,ch->qgh/dot_general | solution.py:61
  72.7 2.1 %multiply_reduce_fusion.1 = (f32[256,2]{0,1:T(2,128)S(1)}, bf16[256,256]{0,1:T(8,128)(2,1)S(1)}) fusion(bf16[256,2,128]{0,2,1:T(8,128)(2,1)S(1)} %fusion.14, bf16[256,2688]{1,0:T(8,128)(2,1)} %all-gather.2.cloned.1.call-done, bf16[256,2688]{1,0:T(8,128)(2,1)S(1)} %copy-done), kind=kOutput, calls=%fused_computation.59 | convolution fusion | flops 352648704 | bytes 3016704 | tf_op jit(solution)/shard_map/nd,hd->nh/dot_general | solution.py:128
  78.5 5.2 %all-to-all-start.2 = ((bf16[4,256,256]{2,1,0:T(8,128)(2,1)}), bf16[4,256,256]{2,1,0:T(8,128)(2,1)}, u32[]{:S(2)}, u32[]{:S(2)}) async-start(bf16[4,256,256]{2,1,0:T(8,128)(2,1)} %bitcast.98), calls=%async_computation.3 | async-start | bytes 1048576 | tf_op jit(solution)/shard_map/all_to_all | solution.py:141
  84.1 2.6 %convolution_convert_fusion = bf16[256,2688]{1,0:T(8,128)(2,1)} fusion(bf16[256,256]{0,1:T(8,128)(2,1)} %bitcast.109, bf16[256,2688]{1,0:T(8,128)(2,1)S(1)} %copy-done), kind=kOutput, calls=%fused_computation | convolution fusion | flops 353009664 | bytes 2883584 | tf_op jit(solution)/shard_map/dot_general | solution.py:136
  86.7 3.0 %all-to-all-done.2 = bf16[4,256,256]{2,1,0:T(8,128)(2,1)} async-done(((bf16[4,256,256]{2,1,0:T(8,128)(2,1)}), bf16[4,256,256]{2,1,0:T(8,128)(2,1)}, u32[]{:S(2)}, u32[]{:S(2)}) %all-to-all-start.2) | async-done | bytes 524320 | tf_op jit(solution)/shard_map/all_to_all | solution.py:141
  89.7 2.1 %fusion.16 = (bf16[256,256]{1,0:T(8,128)(2,1)}, f32[256,256]{1,0:T(8,128)}) fusion(bf16[4,256,256]{2,1,0:T(8,128)(2,1)} %all-to-all-done.2, pred[4]{0:T(512)(128)(4,1)S(1)} %iota_compare_fusion.1), kind=kLoop, calls=%fused_computation.35 | loop fusion | flops 1179648 | bytes 917508 | tf_op jit(solution)/shard_map/reduce_sum | solution.py:144
  91.8 2.1 %collective-permute-start.2 = (bf16[256,256]{1,0:T(8,128)(2,1)}, bf16[256,256]{1,0:T(8,128)(2,1)}, u32[]{:S(2)}, u32[]{:S(2)}) collective-permute-start(bf16[256,256]{1,0:T(8,128)(2,1)} %get-tuple-element.2), channel_id=1, source_target_pairs={{32,0},{64,32},{96,64},{128,96},{160,128},{192,160},{224,192},{256... | collective-permute-start | bytes 393224 | tf_op jit(solution)/shard_map/ppermute | solution.py:24
  94.5 12.3 %collective-permute-done.2 = bf16[256,256]{1,0:T(8,128)(2,1)} collective-permute-done((bf16[256,256]{1,0:T(8,128)(2,1)}, bf16[256,256]{1,0:T(8,128)(2,1)}, u32[]{:S(2)}, u32[]{:S(2)}) %collective-permute-start.2) | collective-permute-done | bytes 131104 | tf_op jit(solution)/shard_map/ppermute | solution.py:24
  111.2 6.9 %collective-permute-start.3 = (bf16[128,2688]{1,0:T(8,128)(2,1)S(1)}, bf16[128,2688]{1,0:T(8,128)(2,1)S(1)}, u32[]{:S(2)}, u32[]{:S(2)}) collective-permute-start(bf16[128,2688]{1,0:T(8,128)(2,1)S(1)} %fusion.2), channel_id=1, source_target_pairs={{0,1},{1,0},{2,3},{3,2},{4,5},{5,4},{6,7},{7,6},{8,9},{9,8},{10,11... | collective-permute-start | bytes 2064392 | tf_op jit(solution)/shard_map/ppermute | solution.py:18
  121.4 9.1 %all-to-all-start.3 = ((bf16[4,32,2688]{2,1,0:T(8,128)(2,1)}), bf16[4,32,2688]{2,1,0:T(8,128)(2,1)S(1)}, u32[]{:S(2)}, u32[]{:S(2)}) async-start(bf16[4,32,2688]{2,1,0:T(8,128)(2,1)} %bitcast.37), calls=%async_computation.4 | async-start | bytes 1376256 | tf_op jit(solution)/shard_map/all_to_all | solution.py:172
  130.5 28.7 %reduce-scatter.2.cloned.1.call-done = bf16[32,2688]{1,0:T(8,128)(2,1)} async-done(((bf16[256,2688]{1,0:T(8,128)(2,1)}), bf16[32,2688]{1,0:T(8,128)(2,1)}) %reduce-scatter.2.cloned.1.call-update) | async-done | bytes 172048 | tf_op jit(solution)/shard_map/reduce_scatter | solution.py:137
  159.2 1.6 add_convert_fusion.2
  (112 shorter events, 18.0 us)
Async XLA Ops:
  7.2 65.5 %copy-start = (bf16[256,2688]{1,0:T(8,128)(2,1)S(1)}, bf16[256,2688]{1,0:T(8,128)(2,1)}, u32[]{:S(2)}) copy-start(bf16[256,2688]{1,0:T(8,128)(2,1)} %param.13) | copy-start | bytes 4128772
  7.2 27.5 %copy-start.4 = (bf16[2688,128]{1,0:T(8,128)(2,1)S(1)}, bf16[2688,128]{1,0:T(8,128)(2,1)}, u32[]{:S(2)}) copy-start(bf16[2688,128]{1,0:T(8,128)(2,1)} %param.11) | copy-start | bytes 2064388
  9.2 19.5 %all-to-all-start = ((bf16[4,32,2688]{2,1,0:T(8,128)(2,1)}), bf16[4,32,2688]{2,1,0:T(8,128)(2,1)S(1)}, u32[]{:S(2)}, u32[]{:S(2)}) async-start(bf16[4,32,2688]{2,1,0:T(8,128)(2,1)} %tile.2), calls=%async_computation | async-start | bytes 1376256 | tf_op jit(solution)/shard_map/all_to_all | solution.py:93
  14.6 58.0 %all-gather.2.cloned.1.call-start = ((), (), s32[]{:S(2)}) async-start(), calls=%async_computation.6 | async-start | bytes 1548288 | tf_op jit(solution)/shard_map/all_gather | solution.py:92
  28.7 5.9 %collective-permute-start = (bf16[128,2688]{1,0:T(8,128)(2,1)S(1)}, bf16[128,2688]{1,0:T(8,128)(2,1)S(1)}, u32[]{:S(2)}, u32[]{:S(2)}) collective-permute-start(bf16[128,2688]{1,0:T(8,128)(2,1)S(1)} %bitcast.103), channel_id=1, source_target_pairs={{0,1},{1,0},{2,3},{3,2},{4,5},{5,4},{6,7},{7,6},{8,9},{9,8},{10,11... | collective-permute-start | bytes 2064392 | tf_op jit(solution)/shard_map/ppermute | solution.py:18
  33.0 28.3 %copy-start.10 = (f32[256,64]{1,0:T(8,128)}, f32[256,64]{1,0:T(8,128)S(1)}, u32[]{:S(2)}) copy-start(f32[256,64]{1,0:T(8,128)S(1)} %get-tuple-element.26) | copy-start | bytes 196612
  33.0 28.3 %copy-start.12 = (f32[256,64]{1,0:T(8,128)}, f32[256,64]{1,0:T(8,128)S(1)}, u32[]{:S(2)}) copy-start(f32[256,64]{1,0:T(8,128)S(1)} %get-tuple-element.27) | copy-start | bytes 196612
  35.7 2.8 %copy-start.8 = (f32[4,2,32,128]{3,2,1,0:T(8,128)}, f32[4,2,32,128]{3,2,1,0:T(8,128)S(1)}, u32[]{:S(2)}) copy-start(f32[4,2,32,128]{3,2,1,0:T(8,128)S(1)} %copy.109) | copy-start | bytes 393220
  36.7 10.7 %copy-start.2 = (bf16[2688,256]{1,0:T(8,128)(2,1)S(1)}, bf16[2688,256]{1,0:T(8,128)(2,1)}, u32[]{:S(2)}) copy-start(bf16[2688,256]{1,0:T(8,128)(2,1)} %param.10) | copy-start | bytes 4128772
  36.7 10.7 %copy-start.20 = (bf16[128,2688]{1,0:T(8,128)(2,1)S(1)}, bf16[128,2688]{1,0:T(8,128)(2,1)}, u32[]{:S(2)}) copy-start(bf16[128,2688]{1,0:T(8,128)(2,1)} %copy-done.19) | copy-start | bytes 2064388
  38.6 15.3 %collective-permute-start.1 = (bf16[256,256]{1,0:T(8,128)(2,1)S(1)}, bf16[256,256]{1,0:T(8,128)(2,1)}, u32[]{:S(2)}, u32[]{:S(2)}) collective-permute-start(bf16[256,256]{1,0:T(8,128)(2,1)S(1)} %pad_maximum_fusion.7), channel_id=1, source_target_pairs={{0,32},{32,64},{64,96},{96,128},{128,160},{160,192},{192,224},{224... | collective-permute-start | bytes 393224 | tf_op jit(solution)/shard_map/ppermute | solution.py:24
  48.0 13.1 %copy-start.17 = (f32[128]{0:T(128)S(1)}, f32[128]{0:T(128)}, u32[]{:S(2)}) copy-start(f32[128]{0:T(128)} %param.14) | copy-start | bytes 1540
  55.8 11.1 %all-to-all-start.1 = ((bf16[4,256,256]{2,1,0:T(8,128)(2,1)}), bf16[4,256,256]{2,1,0:T(8,128)(2,1)S(1)}, u32[]{:S(2)}, u32[]{:S(2)}) async-start(bf16[4,256,256]{2,1,0:T(8,128)(2,1)} %broadcast_select_fusion), calls=%async_computation.1 | async-start | bytes 1048576 | tf_op jit(solution)/shard_map/all_to_all | solution.py:117
  72.6 3.4 %copy-start.16 = (bf16[256,2,128]{0,2,1:T(8,128)(2,1)}, bf16[256,2,128]{0,2,1:T(8,128)(2,1)S(1)}, u32[]{:S(2)}) copy-start(bf16[256,2,128]{0,2,1:T(8,128)(2,1)S(1)} %fusion.14) | copy-start | bytes 393220
  72.6 2.2 %copy-start.1 = (f32[2,256,1280]{1,2,0:T(8,128)S(1)}, f32[2,256,1280]{1,2,0:T(8,128)}, u32[]{:S(2)}) copy-start(f32[2,256,1280]{1,2,0:T(8,128)} %fusion.11) | copy-start | bytes 7864324
  78.5 11.1 %all-to-all-start.2 = ((bf16[4,256,256]{2,1,0:T(8,128)(2,1)}), bf16[4,256,256]{2,1,0:T(8,128)(2,1)}, u32[]{:S(2)}, u32[]{:S(2)}) async-start(bf16[4,256,256]{2,1,0:T(8,128)(2,1)} %bitcast.98), calls=%async_computation.3 | async-start | bytes 1048576 | tf_op jit(solution)/shard_map/all_to_all | solution.py:141
  83.8 75.4 %reduce-scatter.2.cloned.1.call-start = ((), (), s32[]{:S(2)}) async-start(), calls=%async_computation.5 | async-start | bytes 1548288 | tf_op jit(solution)/shard_map/reduce_scatter | solution.py:137
  91.8 14.9 %collective-permute-start.2 = (bf16[256,256]{1,0:T(8,128)(2,1)}, bf16[256,256]{1,0:T(8,128)(2,1)}, u32[]{:S(2)}, u32[]{:S(2)}) collective-permute-start(bf16[256,256]{1,0:T(8,128)(2,1)} %get-tuple-element.2), channel_id=1, source_target_pairs={{32,0},{64,32},{96,64},{128,96},{160,128},{192,160},{224,192},{256... | collective-permute-start | bytes 393224 | tf_op jit(solution)/shard_map/ppermute | solution.py:24
  106.7 1.7 %copy-start.9 = (f32[4,2,32,128]{3,2,1,0:T(8,128)S(1)}, f32[4,2,32,128]{3,2,1,0:T(8,128)}, u32[]{:S(2)}) copy-start(f32[4,2,32,128]{3,2,1,0:T(8,128)} %copy-done.8) | copy-start | bytes 393220
  109.2 1.4 copy-start.3
  111.2 8.7 %collective-permute-start.3 = (bf16[128,2688]{1,0:T(8,128)(2,1)S(1)}, bf16[128,2688]{1,0:T(8,128)(2,1)S(1)}, u32[]{:S(2)}, u32[]{:S(2)}) collective-permute-start(bf16[128,2688]{1,0:T(8,128)(2,1)S(1)} %fusion.2), channel_id=1, source_target_pairs={{0,1},{1,0},{2,3},{3,2},{4,5},{5,4},{6,7},{7,6},{8,9},{9,8},{10,11... | collective-permute-start | bytes 2064392 | tf_op jit(solution)/shard_map/ppermute | solution.py:18
  121.4 37.8 %copy-start.14 = (bf16[32,2688]{1,0:T(8,128)(2,1)S(1)}, bf16[32,2688]{1,0:T(8,128)(2,1)}, u32[]{:S(2)}) copy-start(bf16[32,2688]{1,0:T(8,128)(2,1)} %param.8) | copy-start | bytes 516100
  121.4 39.6 %copy-start.15 = (bf16[32,2688]{1,0:T(8,128)(2,1)S(1)}, bf16[32,2688]{1,0:T(8,128)(2,1)}, u32[]{:S(2)}) copy-start(bf16[32,2688]{1,0:T(8,128)(2,1)} %param.9) | copy-start | bytes 516100
  121.4 39.4 %all-to-all-start.3 = ((bf16[4,32,2688]{2,1,0:T(8,128)(2,1)}), bf16[4,32,2688]{2,1,0:T(8,128)(2,1)S(1)}, u32[]{:S(2)}, u32[]{:S(2)}) async-start(bf16[4,32,2688]{2,1,0:T(8,128)(2,1)} %bitcast.37), calls=%async_computation.4 | async-start | bytes 1376256 | tf_op jit(solution)/shard_map/all_to_all | solution.py:172
  (7 other events, 7.3 us)
Sparse Core Ops, SparseCore 0:
  17.5 44.1 all-gather.1
  94.6 64.6 reduce-scatter.1

commit v2 on v1

v2 whole, which is shorter than its diff:
```python
import functools

import jax
import jax.numpy as jnp
from jax import lax
from jax.experimental import pallas as pl
from jax.experimental.pallas import tpu as pltpu
from jax.sharding import Mesh, PartitionSpec as P

WINDOW = 1024
ALL = ("zh", "x", "y", "zl", "c")
TP = ("zl", "c")

norm_epsilon = 1e-06
score_scale = 168.0 ** (-0.5)
rope_theta = 10000.0
f32 = jnp.float32
bf16 = jnp.bfloat16
i32 = jnp.int32

ROWS = 256
HALF = 128
PIECE = 32
HEAD = 128
Q_HEADS = 2
CHUNKS = 4


def swap_cores(block):
    return lax.ppermute(block, "c", [(0, 1), (1, 0)])


def shift_rows(block, step):
    count = lax.axis_size(("zh", "x"))
    route = [(i, i + step) for i in range(count) if 0 <= i + step < count]
    return lax.ppermute(block, ("zh", "x"), route)


def natural(index):
    return ((index >> 5) & 3) * 64 + (index >> 7) * 32 + (index & 31)


def rope_tables(positions):
    half_size = HEAD // 2
    exponent = jnp.arange(half_size, dtype=f32) * (2.0 / HEAD)
    frequency = jnp.power(f32(rope_theta), -exponent)
    angles = positions.astype(f32)[:, None] * frequency[None, :]
    cosines, sines = jnp.cos(angles), jnp.sin(angles)
    return (
        jnp.concatenate([cosines, cosines], axis=1),
        jnp.concatenate([-sines, sines], axis=1),
    )


def dot_nn(a, b):
    return lax.dot_general(a, b, (((1,), (0,)), ((), ())), preferred_element_type=f32)


def dot_nt(a, b):
    return lax.dot_general(a, b, (((1,), (1,)), ((), ())), preferred_element_type=f32)


def dot_tn(a, b):
    return lax.dot_general(a, b, (((0,), (0,)), ((), ())), preferred_element_type=f32)


def norm_rope(raw, gain, cosines, sines):
    inverse = lax.rsqrt(jnp.mean(raw * raw, axis=-1, keepdims=True) + norm_epsilon)
    normed = raw * inverse * gain
    return normed * cosines + pltpu.roll(normed, HEAD // 2, 1) * sines


def norm_rope_back(raw, gain, cosines, sines, grad):
    inverse = lax.rsqrt(jnp.mean(raw * raw, axis=-1, keepdims=True) + norm_epsilon)
    normed_grad = (grad * cosines - pltpu.roll(grad, HEAD // 2, 1) * sines) * gain
    along = jnp.mean(raw * normed_grad, axis=-1, keepdims=True)
    return inverse * normed_grad - raw * (inverse * inverse * inverse * along)


def copies_kernel(tokens_ref, out_ref):
    for k in range(CHUNKS):
        out_ref[k] = tokens_ref[...]


def kv_kernel(place, mine, other, wk, wv, gain, cos, sin, kv_out, raw_out):
    for rows, which in ((mine, place[0]), (other, 1 - place[0])):
        at = pl.ds(pl.multiple_of(which * HALF, HALF), HALF)
        raw = dot_nn(rows[...], wk[...])
        raw_out[at, :] = raw
        kv_out[at, :HEAD] = norm_rope(raw, gain[...], cos[at, :], sin[at, :]).astype(bf16)
        kv_out[at, HEAD:] = dot_nn(rows[...], wv[...]).astype(bf16)


def q_kernel(place, mine, other, wq, gain, cos, sin, q_out, raw_out):
    for rows, which in ((mine, place[0]), (other, 1 - place[0])):
        at = pl.ds(pl.multiple_of(which * HALF, HALF), HALF)
        raw = dot_nn(rows[...], wq[...])
        raw_out[at, :] = raw
        for h in range(Q_HEADS):
            cols = slice(h * HEAD, (h + 1) * HEAD)
            q_out[at, cols] = norm_rope(raw[:, cols], gain[...], cos[at, :], sin[at, :]).astype(bf16)


def grad_kernel(rows, wo, out):
    got = dot_nt(rows[...], wo[...]).astype(bf16)
    for zl in range(4):
        for c in range(2):
            out[c * HALF + zl * PIECE : c * HALF + (zl + 1) * PIECE, :] = got[
                (zl * 2 + c) * PIECE : (zl * 2 + c + 1) * PIECE, :
            ]


def masks(place, key_axis):
    shape = (ROWS, ROWS)
    ahead = natural(lax.broadcasted_iota(i32, shape, key_axis)) - natural(
        lax.broadcasted_iota(i32, shape, 1 - key_axis)
    )
    everything, nothing = -4 * ROWS, 4 * ROWS
    allowed = []
    for k in range(CHUNKS):
        beyond = jnp.where(place[2] > 0, everything, nothing)
        limit = jnp.where(
            k < place[1], everything, jnp.where((k == place[1]) & (place[2] > 0), 0, beyond)
        )
        allowed.append(ahead > limit)
    allowed.append(ahead <= 0)
    return allowed


def kv_chunk(halo, own, k):
    return halo[k] if k < CHUNKS else own[...]


def forward_kernel(place, q, halo, own, attended_out, probs):
    allowed = masks(place, 1)
    for h in range(Q_HEADS):
        cols = slice(h * HEAD, (h + 1) * HEAD)
        query = q[:, cols]
        total = jnp.zeros((ROWS, 1), f32)
        for k in range(CHUNKS + 1):
            keys = kv_chunk(halo, own, k)[:, :HEAD]
            raw = jnp.where(allowed[k], jnp.exp(dot_nt(query, keys) * score_scale), 0.0)
            total = total + jnp.sum(raw, axis=1, keepdims=True)
            probs[k] = raw
        inverse = 1.0 / total
        result = jnp.zeros((ROWS, HEAD), f32)
        for k in range(CHUNKS + 1):
            low = (probs[k] * inverse).astype(bf16)
            result = result + dot_nn(low, kv_chunk(halo, own, k)[:, HEAD:])
        attended_out[:, cols] = result.astype(bf16)


def out_kernel(attended, wo, out):
    got = dot_nn(attended[...], wo[...]).astype(bf16)
    for zl in range(4):
        for c in range(2):
            out[(zl * 2 + c) * PIECE : (zl * 2 + c + 1) * PIECE, :] = got[
                c * HALF + zl * PIECE : c * HALF + (zl + 1) * PIECE, :
            ]


def backward_kernel(
    place, q, halo, own, grad, attended, q_raw, gain, cos, sin, q_back, halo_back, own_back, probs, dkv
):
    allowed = masks(place, 0)
    for h in range(Q_HEADS):
        cols = slice(h * HEAD, (h + 1) * HEAD)
        query, out_grad = q[:, cols], grad[:, cols]
        products = out_grad.astype(f32) * attended[:, cols].astype(f32)
        dots = jnp.sum(jnp.transpose(products), axis=0, keepdims=True)
        total = jnp.zeros((1, ROWS), f32)
        for k in range(CHUNKS + 1):
            keys = kv_chunk(halo, own, k)[:, :HEAD]
            raw = jnp.where(allowed[k], jnp.exp(dot_nt(keys, query) * score_scale), 0.0)
            total = total + jnp.sum(raw, axis=0, keepdims=True)
            probs[k] = raw
        inverse = 1.0 / total
        query_grad = jnp.zeros((ROWS, HEAD), f32)
        for k in range(CHUNKS + 1):
            kv = kv_chunk(halo, own, k)
            soft = probs[k] * inverse
            prob_grad = dot_nt(kv[:, HEAD:], out_grad)
            score_grad = (soft * (prob_grad - dots) * score_scale).astype(bf16)
            value_grad = dot_nn(soft.astype(bf16), out_grad)
            key_grad = dot_nn(score_grad, query)
            query_grad = query_grad + dot_tn(score_grad, kv[:, :HEAD])
            if h > 0:
                key_grad = key_grad + dkv[k, :, :HEAD]
                value_grad = value_grad + dkv[k, :, HEAD:]
            if h < Q_HEADS - 1:
                dkv[k, :, :HEAD] = key_grad
                dkv[k, :, HEAD:] = value_grad
            elif k < CHUNKS:
                halo_back[k, :, :HEAD] = key_grad.astype(bf16)
                halo_back[k, :, HEAD:] = value_grad.astype(bf16)
            else:
                own_back[:, :HEAD] = key_grad
                own_back[:, HEAD:] = value_grad
        q_back[:, cols] = norm_rope_back(
            q_raw[:, cols], gain[...], cos[...], sin[...], query_grad
        ).astype(bf16)


def gather_kernel(place, back, own_back, own_out, above_out):
    own = own_back[...]
    above = jnp.zeros((ROWS, 2 * HEAD), f32)
    for k in range(CHUNKS):
        later = k > place[1]
        piece = back[k].astype(f32)
        own = own + jnp.where(later, piece, 0.0)
        above = above + jnp.where(later, 0.0, piece)
    own_out[...] = own
    above_out[...] = above.astype(bf16)


def base_kernel(q_back, wq, out):
    out[...] = dot_nt(q_back[...], wq[...])


def end_rows(place, which, base, own, below, k_raw, gain, cos, sin, wk, wv):
    at = pl.ds(pl.multiple_of(which * HALF, HALF), HALF)
    total = own[at, :] + below[at, :].astype(f32)
    key_back = norm_rope_back(k_raw[at, :], gain[...], cos[at, :], sin[at, :], total[:, :HEAD])
    return (
        base[at, :]
        + dot_nt(key_back.astype(bf16), wk[...])
        + dot_nt(total[:, HEAD:].astype(bf16), wv[...])
    )


def end_given_kernel(place, base, own, below, k_raw, gain, cos, sin, wk, wv, given):
    given[...] = end_rows(
        place, 1 - place[0], base, own, below, k_raw, gain, cos, sin, wk, wv
    ).astype(bf16)


def end_pair_kernel(place, base, own, below, k_raw, gain, cos, sin, wk, wv, arrived, pair):
    rows = end_rows(place, place[0], base, own, below, k_raw, gain, cos, sin, wk, wv)
    pair[...] = (rows + arrived[...].astype(f32)).astype(bf16)


def sum_kernel(first, pieces, out):
    total = first[...].astype(f32)
    for k in range(CHUNKS):
        total = total + pieces[k].astype(f32)
    out[...] = total.astype(bf16)


def call(kernel, outs, *operands, scratch=(), flops=0):
    in_specs = [
        pl.BlockSpec(memory_space=pltpu.SMEM if a.dtype == i32 else pltpu.VMEM) for a in operands
    ]
    shapes = [jax.ShapeDtypeStruct(shape, dtype) for shape, dtype in outs]
    size = sum(a.size * a.dtype.itemsize for a in (*operands, *shapes))
    results = pl.pallas_call(
        kernel,
        out_shape=shapes,
        in_specs=in_specs,
        out_specs=[pl.BlockSpec(memory_space=pltpu.VMEM)] * len(shapes),
        scratch_shapes=scratch,
        compiler_params=pltpu.CompilerParams(vmem_limit_bytes=8 * 2**20),
        cost_estimate=pl.CostEstimate(flops=flops, bytes_accessed=size, transcendentals=0),
        name=kernel.__name__,
    )(*operands)
    return results[0] if len(results) == 1 else results


def on_device(
    tokens, result_grad, query_weight, key_weight, value_weight, output_weight, query_gain, key_gain
):
    width = tokens.shape[1]
    core, y = lax.axis_index("c"), lax.axis_index("y")
    block_row = lax.axis_index(("zh", "x"))
    place = jnp.stack([core, y, block_row]).astype(i32)
    query_gain, key_gain = query_gain[None], key_gain[None]
    positions = (block_row * CHUNKS + y) * ROWS + natural(jnp.arange(ROWS, dtype=i32))
    cos, sin = rope_tables(positions)

    gradients_part = lax.all_gather(result_grad, TP, axis=0, tiled=True)
    copies = call(copies_kernel, [((CHUNKS, PIECE, width), bf16)], tokens)
    mine = lax.all_to_all(copies, "zl", 0, 0, tiled=True).reshape(HALF, width)
    other = swap_cores(mine)
    own_kv, key_raw = call(
        kv_kernel,
        [((ROWS, 2 * HEAD), bf16), ((ROWS, HEAD), f32)],
        place, mine, other, key_weight, value_weight, key_gain, cos, sin,
    )
    above_kv = shift_rows(own_kv, 1)
    queries, query_raw = call(
        q_kernel,
        [((ROWS, Q_HEADS * HEAD), bf16), ((ROWS, Q_HEADS * HEAD), f32)],
        place, mine, other, query_weight, query_gain, cos, sin,
    )
    targets = jnp.arange(CHUNKS, dtype=i32)
    outgoing = jnp.where((targets > y)[:, None, None], own_kv[None], above_kv[None])
    halo = lax.all_to_all(outgoing, "y", 0, 0, tiled=True)
    out_grad = call(
        grad_kernel, [((ROWS, Q_HEADS * HEAD), bf16)], gradients_part, output_weight
    )
    probs = pltpu.VMEM((CHUNKS + 1, ROWS, ROWS), f32)
    attended = call(
        forward_kernel, [((ROWS, Q_HEADS * HEAD), bf16)], place, queries, halo, own_kv, scratch=[probs]
    )
    out_part = call(out_kernel, [((ROWS, width), bf16)], attended, output_weight)
    out_sum = lax.psum_scatter(out_part, TP, scatter_dimension=0, tiled=True)
    query_back, halo_back, own_back = call(
        backward_kernel,
        [
            ((ROWS, Q_HEADS * HEAD), bf16),
            ((CHUNKS, ROWS, 2 * HEAD), bf16),
            ((ROWS, 2 * HEAD), f32),
        ],
        place, queries, halo, own_kv, out_grad, attended, query_raw, query_gain, cos, sin,
        scratch=[probs, pltpu.VMEM((CHUNKS + 1, ROWS, 2 * HEAD), f32)],
    )
    back = lax.all_to_all(halo_back, "y", 0, 0, tiled=True)
    own_sum, above_sum = call(
        gather_kernel,
        [((ROWS, 2 * HEAD), f32), ((ROWS, 2 * HEAD), bf16)],
        place, back, own_back,
    )
    below = shift_rows(above_sum, -1)
    base = call(base_kernel, [((ROWS, width), f32)], query_back, query_weight)
    last = (place, base, own_sum, below, key_raw, key_gain, cos, sin, key_weight, value_weight)
    given = swap_cores(call(end_given_kernel, [((HALF, width), bf16)], *last))
    pair = call(end_pair_kernel, [((HALF, width), bf16)], *last, given)
    pieces = lax.all_to_all(pair.reshape(CHUNKS, PIECE, width), "zl", 0, 0, tiled=True)
    layer_output = (tokens.astype(f32) + out_sum.astype(f32)).astype(bf16)
    tokens_grad = call(sum_kernel, [((PIECE, width), bf16)], result_grad, pieces)
    return (layer_output, tokens_grad)


def solution(mesh):
    fine = Mesh(mesh.devices.reshape(4, 4, 4, 4, 2), ALL)
    in_specs = (
        P(ALL, None),
        P(ALL, None),
        P(None, TP),
        P(None, TP),
        P(None, TP),
        P(TP, None),
        P(),
        P(),
    )
    out_specs = (P(ALL, None), P(ALL, None))
    return jax.shard_map(
        on_device, mesh=fine, in_specs=in_specs, out_specs=out_specs, check_vma=False
    )
```

time: 169 us -> 159 us (0.941)
  the two profiles are of different devices: /device:TPU:47 before, /device:TPU:6 now
where the time goes in v2:
time: 159 us; the launch traced here: 158 us
  waiting for transfers between devices  56.5 us (36%)
  starting transfers between devices  43 us (27%)
  Pallas kernels  17.3 us (11%)
  between operations  14.3 us (9%)
  local copies, waits for them, and re-layouts  12.6 us (8%)
  blocking collectives  11.4 us (7%)
  other arithmetic  3.33 us (2%)
    all_to_all x1, starting transfers between devices, on_device(): lax.all_to_all(pair.reshape(CHUNKS, PIECE, width), 'zl', 0, 0, tiled=True)  17.5 us
    pallas_call x12, Pallas kernels, call(): pl.pallas_call(kernel, out_shape=shapes, in_specs=in_specs, out_specs=[pl...  17.3 us
    all_to_all x1, waiting for transfers between devices, on_device(): mine = lax.all_to_all(copies, 'zl', 0, 0, tiled=True).reshape(HALF, width)  17.3 us
    ppermute x2, waiting for transfers between devices, shift_rows(): return lax.ppermute(block, ('zh', 'x'), route)  17.1 us
    all_to_all x1, waiting for transfers between devices, on_device(): lax.all_to_all(pair.reshape(CHUNKS, PIECE, width), 'zl', 0, 0, tiled=True)  16.7 us
    unnamed x60, local copies, waits for them, and re-layouts  12.6 us
    all_to_all x1, blocking collectives, on_device(): back = lax.all_to_all(halo_back, 'y', 0, 0, tiled=True)  11.4 us
    ppermute x2, starting transfers between devices, shift_rows(): return lax.ppermute(block, ('zh', 'x'), route)  11.1 us
  transfers between devices with their start and end apart: 9, of which 7 were waited for; matrix products, arithmetic and copies ran while one was open for 2% of the time, Pallas kernels for 10%

profile of v2, /device:TPU:6, one launch (start us, length us, event | category | flops | bytes accessed | tf_op | source)
XLA Modules:
  0.0 158.5 jit_solution(3932881951709802178)
XLA Ops:
  9.0 6.0 %all-to-all-start = ((bf16[4,32,2688]{2,1,0:T(8,128)(2,1)}), bf16[4,32,2688]{2,1,0:T(8,128)(2,1)S(1)}, u32[]{:S(2)}, u32[]{:S(2)}) async-start(bf16[4,32,2688]{2,1,0:T(8,128)(2,1)} %copies_kernel.1), calls=%async_computation | async-start | bytes 1376256 | tf_op jit(solution)/shard_map/all_to_all | solution.py:281
  15.8 17.3 %all-to-all-done = bf16[4,32,2688]{2,1,0:T(8,128)(2,1)S(1)} async-done(((bf16[4,32,2688]{2,1,0:T(8,128)(2,1)}), bf16[4,32,2688]{2,1,0:T(8,128)(2,1)S(1)}, u32[]{:S(2)}, u32[]{:S(2)}) %all-to-all-start) | async-done | bytes 688160 | tf_op jit(solution)/shard_map/all_to_all | solution.py:281
  33.0 1.9 %collective-permute-start = (bf16[128,2688]{1,0:T(8,128)(2,1)S(1)}, bf16[128,2688]{1,0:T(8,128)(2,1)S(1)}, u32[]{:S(2)}, u32[]{:S(2)}) collective-permute-start(bf16[128,2688]{1,0:T(8,128)(2,1)S(1)} %bitcast.7), channel_id=1, source_target_pairs={{0,1},{1,0},{2,3},{3,2},{4,5},{5,4},{6,7},{7,6},{8,9},{9,8},{10,11... | collective-permute-start | bytes 2064392 | tf_op jit(solution)/shard_map/ppermute | solution.py:30
  35.8 1.3 collective-permute-done.other
  37.1 1.5 kv_kernel.1
  39.2 9.1 %collective-permute-start.1 = (bf16[256,256]{1,0:T(8,128)(2,1)S(1)}, bf16[256,256]{1,0:T(8,128)(2,1)S(1)}, u32[]{:S(2)}, u32[]{:S(2)}) collective-permute-start(bf16[256,256]{1,0:T(8,128)(2,1)S(1)} %get-tuple-element.12.own), channel_id=1, source_target_pairs={{0,32},{32,64},{64,96},{96,128},{128,160},{160,192},{192,224},{224... | collective-permute-start | bytes 393224 | tf_op jit(solution)/shard_map/ppermute | solution.py:36
  48.4 5.4 %collective-permute-done.1 = bf16[256,256]{1,0:T(8,128)(2,1)S(1)} collective-permute-done((bf16[256,256]{1,0:T(8,128)(2,1)S(1)}, bf16[256,256]{1,0:T(8,128)(2,1)S(1)}, u32[]{:S(2)}, u32[]{:S(2)}) %collective-permute-start.1) | collective-permute-done | bytes 131104 | tf_op jit(solution)/shard_map/ppermute | solution.py:36
  55.4 4.6 %all-to-all-start.1 = ((bf16[4,256,256]{2,1,0:T(8,128)(2,1)}), bf16[4,256,256]{2,1,0:T(8,128)(2,1)}, u32[]{:S(2)}, u32[]{:S(2)}) async-start(bf16[4,256,256]{2,1,0:T(8,128)(2,1)} %broadcast_select_fusion), calls=%async_computation.1 | async-start | bytes 1048576 | tf_op jit(solution)/shard_map/all_to_all | solution.py:296
  60.1 1.3 copy-done.3
  64.3 1.3 q_kernel.1
  66.9 1.3 all-to-all-done.1.halo
  70.0 2.4 %forward_kernel.1.attended = bf16[256,256]{1,0:T(8,128)(2,1)S(1)} custom-call(s32[3]{0:T(128)S(1)} %pad_add_fusion.place, bf16[256,256]{1,0:T(8,128)(2,1)S(1)} %copy-done.22, bf16[4,256,256]{2,1,0:T(8,128)(2,1)} %all-to-all-done.1.halo, bf16[256,256]{1,0:T(8,128)(2,1)S(1)} %copy-done.16), custom_call_target="tpu_custom_call" | custom-call | bytes 917516 | tf_op jit(solution)/shard_map/forward_kernel/pallas_call | solution.py:255
  74.2 1.4 copy-done.14
  76.7 4.6 %backward_kernel.1 = (bf16[256,256]{1,0:T(8,128)(2,1)S(1)}, bf16[4,256,256]{2,1,0:T(8,128)(2,1)S(1)}, f32[256,256]{1,0:T(8,128)S(1)}) custom-call(s32[3]{0:T(128)S(1)} %pad_add_fusion.place, bf16[256,256]{1,0:T(8,128)(2,1)S(1)} %copy-done.23, bf16[4,256,256]{2,1,0:T(8,128)(2,1)} %all-to-all-done.1.halo, bf16[256,256]{1,0:T(8,128)(2,1)S(1)} %copy-done.17, ...), custom_call_target="tpu_custom_call" | custom-call | bytes 2490892 | tf_op jit(solution)/shard_map/backward_kernel/pallas_call | solution.py:255
  81.4 11.4 %all_to_all.20.back = bf16[4,256,256]{2,1,0:T(8,128)(2,1)S(1)} all-to-all(bf16[4,256,256]{2,1,0:T(8,128)(2,1)S(1)} %get-tuple-element.15), channel_id=1, replica_groups=mesh['zh'=4,'x'=4,'y'=4,'zl'=4,'c'=2] {'y'}, dimensions={0} | all-to-all | bytes 1048576 | tf_op jit(solution)/shard_map/all_to_all | solution.py:316
  93.5 1.9 %collective-permute-start.2 = (bf16[256,256]{1,0:T(8,128)(2,1)S(1)}, bf16[256,256]{1,0:T(8,128)(2,1)S(1)}, u32[]{:S(2)}, u32[]{:S(2)}) collective-permute-start(bf16[256,256]{1,0:T(8,128)(2,1)S(1)} %get-tuple-element.18), channel_id=1, source_target_pairs={{32,0},{64,32},{96,64},{128,96},{160,128},{192,160},{224,192},{256... | collective-permute-start | bytes 393224 | tf_op jit(solution)/shard_map/ppermute | solution.py:36
  96.0 11.6 %collective-permute-done.2.below = bf16[256,256]{1,0:T(8,128)(2,1)S(1)} collective-permute-done((bf16[256,256]{1,0:T(8,128)(2,1)S(1)}, bf16[256,256]{1,0:T(8,128)(2,1)S(1)}, u32[]{:S(2)}, u32[]{:S(2)}) %collective-permute-start.2) | collective-permute-done | bytes 131104 | tf_op jit(solution)/shard_map/ppermute | solution.py:36
  107.7 1.2 end_given_kernel.1
  108.9 1.9 %collective-permute-start.3 = (bf16[128,2688]{1,0:T(8,128)(2,1)S(1)}, bf16[128,2688]{1,0:T(8,128)(2,1)S(1)}, u32[]{:S(2)}, u32[]{:S(2)}) collective-permute-start(bf16[128,2688]{1,0:T(8,128)(2,1)S(1)} %end_given_kernel.1), channel_id=1, source_target_pairs={{0,1},{1,0},{2,3},{3,2},{4,5},{5,4},{6,7},{7,6},{8,9},{9,8},{10,11... | collective-permute-start | bytes 2064392 | tf_op jit(solution)/shard_map/ppermute | solution.py:30
  110.8 2.1 %collective-permute-done.3.arrived = bf16[128,2688]{1,0:T(8,128)(2,1)S(1)} collective-permute-done((bf16[128,2688]{1,0:T(8,128)(2,1)S(1)}, bf16[128,2688]{1,0:T(8,128)(2,1)S(1)}, u32[]{:S(2)}, u32[]{:S(2)}) %collective-permute-start.3) | collective-permute-done | bytes 688160 | tf_op jit(solution)/shard_map/ppermute | solution.py:30
  113.0 2.1 %end_pair_kernel.1 = bf16[128,2688]{1,0:T(8,128)(2,1)} custom-call(s32[3]{0:T(128)S(1)} %pad_add_fusion.place, f32[256,2688]{1,0:T(8,128)S(1)} %base_kernel.1.base, f32[256,256]{1,0:T(8,128)S(1)} %get-tuple-element.17.own, bf16[256,256]{1,0:T(8,128)(2,1)S(1)} %collective-permute-done.2.below, f32[256,128]{1,0:T(8,128)S(1)} %copy-done.25, ...), custom_call_target="tpu_custom_call" | custom-call | bytes 6291980 | tf_op jit(solution)/shard_map/end_pair_kernel/pallas_call | solution.py:255
  115.1 17.5 %all-to-all-start.3 = ((bf16[4,32,2688]{2,1,0:T(8,128)(2,1)}), bf16[4,32,2688]{2,1,0:T(8,128)(2,1)S(1)}, u32[]{:S(2)}, u32[]{:S(2)}) async-start(bf16[4,32,2688]{2,1,0:T(8,128)(2,1)} %bitcast.6), calls=%async_computation.4 | async-start | bytes 1376256 | tf_op jit(solution)/shard_map/all_to_all | solution.py:327
  132.6 1.6 %add_convert_fusion = bf16[32,2688]{1,0:T(8,128)(2,1)} fusion(bf16[32,2688]{1,0:T(8,128)(2,1)} %reduce-scatter.2.cloned.1.call-done, bf16[32,2688]{1,0:T(8,128)(2,1)S(1)} %copy-done.19), kind=kLoop, calls=%fused_computation.1 | loop fusion | flops 344064 | bytes 516096 | tf_op jit(solution)/shard_map/convert_element_type | solution.py:328
  134.2 16.7 %all-to-all-done.3.pieces = bf16[4,32,2688]{2,1,0:T(8,128)(2,1)S(1)} async-done(((bf16[4,32,2688]{2,1,0:T(8,128)(2,1)}), bf16[4,32,2688]{2,1,0:T(8,128)(2,1)S(1)}, u32[]{:S(2)}, u32[]{:S(2)}) %all-to-all-start.3) | async-done | bytes 688160 | tf_op jit(solution)/shard_map/all_to_all | solution.py:327
  (77 shorter events, 16.5 us)
Async XLA Ops:
  9.0 28.1 %copy-start = (bf16[2688,128]{1,0:T(8,128)(2,1)S(1)}, bf16[2688,128]{1,0:T(8,128)(2,1)}, u32[]{:S(2)}) copy-start(bf16[2688,128]{1,0:T(8,128)(2,1)} %wk.5) | copy-start | bytes 2064388
  9.0 28.1 %copy-start.1 = (bf16[2688,128]{1,0:T(8,128)(2,1)S(1)}, bf16[2688,128]{1,0:T(8,128)(2,1)}, u32[]{:S(2)}) copy-start(bf16[2688,128]{1,0:T(8,128)(2,1)} %wv.5) | copy-start | bytes 2064388
  9.0 28.1 %copy-start.28 = (f32[128]{0:T(128)S(1)}, f32[128]{0:T(128)}, u32[]{:S(2)}) copy-start(f32[128]{0:T(128)} %param.15) | copy-start | bytes 1540
  9.0 24.0 %all-to-all-start = ((bf16[4,32,2688]{2,1,0:T(8,128)(2,1)}), bf16[4,32,2688]{2,1,0:T(8,128)(2,1)S(1)}, u32[]{:S(2)}, u32[]{:S(2)}) async-start(bf16[4,32,2688]{2,1,0:T(8,128)(2,1)} %copies_kernel.1), calls=%async_computation | async-start | bytes 1376256 | tf_op jit(solution)/shard_map/all_to_all | solution.py:281
  15.0 59.2 %all-gather.2.cloned.1.call-start = ((), (), s32[]{:S(2)}) async-start(), calls=%async_computation.6 | async-start | bytes 1548288 | tf_op jit(solution)/shard_map/all_gather | solution.py:279
  33.0 4.0 %collective-permute-start = (bf16[128,2688]{1,0:T(8,128)(2,1)S(1)}, bf16[128,2688]{1,0:T(8,128)(2,1)S(1)}, u32[]{:S(2)}, u32[]{:S(2)}) collective-permute-start(bf16[128,2688]{1,0:T(8,128)(2,1)S(1)} %bitcast.7), channel_id=1, source_target_pairs={{0,1},{1,0},{2,3},{3,2},{4,5},{5,4},{6,7},{7,6},{8,9},{9,8},{10,11... | collective-permute-start | bytes 2064392 | tf_op jit(solution)/shard_map/ppermute | solution.py:30
  35.7 2.8 %copy-start.6 = (f32[256,128]{1,0:T(8,128)}, f32[256,128]{1,0:T(8,128)S(1)}, u32[]{:S(2)}) copy-start(f32[256,128]{1,0:T(8,128)S(1)} %get-tuple-element.23.cos) | copy-start | bytes 393220
  35.8 2.8 %copy-start.9 = (f32[256,128]{1,0:T(8,128)}, f32[256,128]{1,0:T(8,128)S(1)}, u32[]{:S(2)}) copy-start(f32[256,128]{1,0:T(8,128)S(1)} %get-tuple-element.24.sin) | copy-start | bytes 393220
  37.1 1.5 copy-start.12
  39.2 20.8 %copy-start.29 = (f32[128]{0:T(128)S(1)}, f32[128]{0:T(128)}, u32[]{:S(2)}) copy-start(f32[128]{0:T(128)} %param.14) | copy-start | bytes 1540
  39.2 14.6 %collective-permute-start.1 = (bf16[256,256]{1,0:T(8,128)(2,1)S(1)}, bf16[256,256]{1,0:T(8,128)(2,1)S(1)}, u32[]{:S(2)}, u32[]{:S(2)}) collective-permute-start(bf16[256,256]{1,0:T(8,128)(2,1)S(1)} %get-tuple-element.12.own), channel_id=1, source_target_pairs={{0,32},{32,64},{64,96},{96,128},{128,160},{160,192},{192,224},{224... | collective-permute-start | bytes 393224 | tf_op jit(solution)/shard_map/ppermute | solution.py:36
  55.4 12.8 %all-to-all-start.1 = ((bf16[4,256,256]{2,1,0:T(8,128)(2,1)}), bf16[4,256,256]{2,1,0:T(8,128)(2,1)}, u32[]{:S(2)}, u32[]{:S(2)}) async-start(bf16[4,256,256]{2,1,0:T(8,128)(2,1)} %broadcast_select_fusion), calls=%async_computation.1 | async-start | bytes 1048576 | tf_op jit(solution)/shard_map/all_to_all | solution.py:296
  60.0 72.5 %reduce-scatter.2.cloned.1.call-start = ((), (), s32[]{:S(2)}) async-start(), calls=%async_computation.5 | async-start | bytes 1548288 | tf_op jit(solution)/shard_map/reduce_scatter | solution.py:305
  64.3 8.2 %copy-start.2 = (bf16[256,2688]{1,0:T(8,128)(2,1)S(1)}, bf16[256,2688]{1,0:T(8,128)(2,1)}, u32[]{:S(2)}) copy-start(bf16[256,2688]{1,0:T(8,128)(2,1)} %wo.3) | copy-start | bytes 4128772
  74.2 2.0 %copy-start.8 = (f32[256,128]{1,0:T(8,128)S(1)}, f32[256,128]{1,0:T(8,128)}, u32[]{:S(2)}) copy-start(f32[256,128]{1,0:T(8,128)} %copy-done.6) | copy-start | bytes 393220
  74.2 2.0 %copy-start.11 = (f32[256,128]{1,0:T(8,128)S(1)}, f32[256,128]{1,0:T(8,128)}, u32[]{:S(2)}) copy-start(f32[256,128]{1,0:T(8,128)} %copy-done.9) | copy-start | bytes 393220
  74.2 1.4 copy-start.14
  76.7 18.7 %copy-start.4 = (bf16[2688,256]{1,0:T(8,128)(2,1)S(1)}, bf16[2688,256]{1,0:T(8,128)(2,1)}, u32[]{:S(2)}) copy-start(bf16[2688,256]{1,0:T(8,128)(2,1)} %wq.3) | copy-start | bytes 4128772
  93.5 14.2 %collective-permute-start.2 = (bf16[256,256]{1,0:T(8,128)(2,1)S(1)}, bf16[256,256]{1,0:T(8,128)(2,1)S(1)}, u32[]{:S(2)}, u32[]{:S(2)}) collective-permute-start(bf16[256,256]{1,0:T(8,128)(2,1)S(1)} %get-tuple-element.18), channel_id=1, source_target_pairs={{32,0},{64,32},{96,64},{128,96},{160,128},{192,160},{224,192},{256... | collective-permute-start | bytes 393224 | tf_op jit(solution)/shard_map/ppermute | solution.py:36
  95.4 12.2 %copy-start.25 = (f32[256,128]{1,0:T(8,128)S(1)}, f32[256,128]{1,0:T(8,128)}, u32[]{:S(2)}) copy-start(f32[256,128]{1,0:T(8,128)} %copy-done.24) | copy-start | bytes 393220
  108.9 4.1 %collective-permute-start.3 = (bf16[128,2688]{1,0:T(8,128)(2,1)S(1)}, bf16[128,2688]{1,0:T(8,128)(2,1)S(1)}, u32[]{:S(2)}, u32[]{:S(2)}) collective-permute-start(bf16[128,2688]{1,0:T(8,128)(2,1)S(1)} %end_given_kernel.1), channel_id=1, source_target_pairs={{0,1},{1,0},{2,3},{3,2},{4,5},{5,4},{6,7},{7,6},{8,9},{9,8},{10,11... | collective-permute-start | bytes 2064392 | tf_op jit(solution)/shard_map/ppermute | solution.py:30
  115.1 17.5 %copy-start.19 = (bf16[32,2688]{1,0:T(8,128)(2,1)S(1)}, bf16[32,2688]{1,0:T(8,128)(2,1)}, u32[]{:S(2)}) copy-start(bf16[32,2688]{1,0:T(8,128)(2,1)} %tokens_ref.1) | copy-start | bytes 516100
  115.1 35.8 %copy-start.20 = (bf16[32,2688]{1,0:T(8,128)(2,1)S(1)}, bf16[32,2688]{1,0:T(8,128)(2,1)}, u32[]{:S(2)}) copy-start(bf16[32,2688]{1,0:T(8,128)(2,1)} %first.1) | copy-start | bytes 516100
  115.1 35.8 %all-to-all-start.3 = ((bf16[4,32,2688]{2,1,0:T(8,128)(2,1)}), bf16[4,32,2688]{2,1,0:T(8,128)(2,1)S(1)}, u32[]{:S(2)}, u32[]{:S(2)}) async-start(bf16[4,32,2688]{2,1,0:T(8,128)(2,1)} %bitcast.6), calls=%async_computation.4 | async-start | bytes 1376256 | tf_op jit(solution)/shard_map/all_to_all | solution.py:327
  (15 other events, 13.6 us)
Sparse Core Ops, SparseCore 0:
  17.9 48.1 all-gather.1
  74.3 51.2 reduce-scatter.1

commit v3 on v2

--- a/solution.py
+++ b/solution.py
@@ -24,6 +24,8 @@
 HEAD = 128
 Q_HEADS = 2
 CHUNKS = 4
+BLOCKED = True
+VMEM_MIB = 20
 
 
 def swap_cores(block):
@@ -131,25 +133,6 @@
     return halo[k] if k < CHUNKS else own[...]
 
 
-def forward_kernel(place, q, halo, own, attended_out, probs):
-    allowed = masks(place, 1)
-    for h in range(Q_HEADS):
-        cols = slice(h * HEAD, (h + 1) * HEAD)
-        query = q[:, cols]
-        total = jnp.zeros((ROWS, 1), f32)
-        for k in range(CHUNKS + 1):
-            keys = kv_chunk(halo, own, k)[:, :HEAD]
-            raw = jnp.where(allowed[k], jnp.exp(dot_nt(query, keys) * score_scale), 0.0)
-            total = total + jnp.sum(raw, axis=1, keepdims=True)
-            probs[k] = raw
-        inverse = 1.0 / total
-        result = jnp.zeros((ROWS, HEAD), f32)
-        for k in range(CHUNKS + 1):
-            low = (probs[k] * inverse).astype(bf16)
-            result = result + dot_nn(low, kv_chunk(halo, own, k)[:, HEAD:])
-        attended_out[:, cols] = result.astype(bf16)
-
-
 def out_kernel(attended, wo, out):
     got = dot_nn(attended[...], wo[...]).astype(bf16)
     for zl in range(4):
@@ -159,15 +142,14 @@
             ]
 
 
-def backward_kernel(
-    place, q, halo, own, grad, attended, q_raw, gain, cos, sin, q_back, halo_back, own_back, probs, dkv
+def attention_kernel(
+    place, q, halo, own, grad, q_raw, gain, cos, sin,
+    attended_out, q_back, halo_back, own_back, probs, dkv,
 ):
     allowed = masks(place, 0)
     for h in range(Q_HEADS):
         cols = slice(h * HEAD, (h + 1) * HEAD)
         query, out_grad = q[:, cols], grad[:, cols]
-        products = out_grad.astype(f32) * attended[:, cols].astype(f32)
-        dots = jnp.sum(jnp.transpose(products), axis=0, keepdims=True)
         total = jnp.zeros((1, ROWS), f32)
         for k in range(CHUNKS + 1):
             keys = kv_chunk(halo, own, k)[:, :HEAD]
@@ -175,29 +157,41 @@
             total = total + jnp.sum(raw, axis=0, keepdims=True)
             probs[k] = raw
         inverse = 1.0 / total
-        query_grad = jnp.zeros((ROWS, HEAD), f32)
+        attended = jnp.zeros((HEAD, ROWS), f32)
+        for k in range(CHUNKS + 1):
+            soft = probs[k] * inverse
+            probs[k] = soft
+            low = soft.astype(bf16)
+            attended = attended + dot_tn(kv_chunk(halo, own, k)[:, HEAD:], low)
+            value_grad = dot_nn(low, out_grad)
+            if h > 0:
+                value_grad = value_grad + dkv[k, :, HEAD:]
+            if h < Q_HEADS - 1:
+                dkv[k, :, HEAD:] = value_grad
+            elif k < CHUNKS:
+                halo_back[k, :, HEAD:] = value_grad.astype(bf16)
+            else:
+                own_back[:, HEAD:] = value_grad
+        attended_out[:, cols] = jnp.transpose(attended).astype(bf16)
+        products = jnp.transpose(out_grad.astype(f32)) * attended.astype(bf16).astype(f32)
+        dots = jnp.sum(products, axis=0, keepdims=True)
+        query_grad = jnp.zeros((HEAD, ROWS), f32)
         for k in range(CHUNKS + 1):
             kv = kv_chunk(halo, own, k)
-            soft = probs[k] * inverse
             prob_grad = dot_nt(kv[:, HEAD:], out_grad)
-            score_grad = (soft * (prob_grad - dots) * score_scale).astype(bf16)
-            value_grad = dot_nn(soft.astype(bf16), out_grad)
+            score_grad = (probs[k] * (prob_grad - dots) * score_scale).astype(bf16)
             key_grad = dot_nn(score_grad, query)
-            query_grad = query_grad + dot_tn(score_grad, kv[:, :HEAD])
+            query_grad = query_grad + dot_tn(kv[:, :HEAD], score_grad)
             if h > 0:
                 key_grad = key_grad + dkv[k, :, :HEAD]
-                value_grad = value_grad + dkv[k, :, HEAD:]
             if h < Q_HEADS - 1:
                 dkv[k, :, :HEAD] = key_grad
-                dkv[k, :, HEAD:] = value_grad
             elif k < CHUNKS:
                 halo_back[k, :, :HEAD] = key_grad.astype(bf16)
-                halo_back[k, :, HEAD:] = value_grad.astype(bf16)
             else:
                 own_back[:, :HEAD] = key_grad
-                own_back[:, HEAD:] = value_grad
         q_back[:, cols] = norm_rope_back(
-            q_raw[:, cols], gain[...], cos[...], sin[...], query_grad
+            q_raw[:, cols], gain[...], cos[...], sin[...], jnp.transpose(query_grad)
         ).astype(bf16)
 
 
@@ -251,14 +245,24 @@
         pl.BlockSpec(memory_space=pltpu.SMEM if a.dtype == i32 else pltpu.VMEM) for a in operands
     ]
     shapes = [jax.ShapeDtypeStruct(shape, dtype) for shape, dtype in outs]
+    out_specs = [pl.BlockSpec(memory_space=pltpu.VMEM)] * len(shapes)
+    grid = ()
+    if BLOCKED:
+        whole = lambda a: pl.BlockSpec(a.shape, lambda i: (0,) * len(a.shape))
+        in_specs = [
+            pl.BlockSpec(memory_space=pltpu.SMEM) if a.dtype == i32 else whole(a) for a in operands
+        ]
+        out_specs = [whole(a) for a in shapes]
+        grid = (1,)
     size = sum(a.size * a.dtype.itemsize for a in (*operands, *shapes))
     results = pl.pallas_call(
         kernel,
         out_shape=shapes,
         in_specs=in_specs,
-        out_specs=[pl.BlockSpec(memory_space=pltpu.VMEM)] * len(shapes),
+        out_specs=out_specs,
+        grid=grid,
         scratch_shapes=scratch,
-        compiler_params=pltpu.CompilerParams(vmem_limit_bytes=8 * 2**20),
+        compiler_params=pltpu.CompilerParams(vmem_limit_bytes=VMEM_MIB * 2**20),
         cost_estimate=pl.CostEstimate(flops=flops, bytes_accessed=size, transcendentals=0),
         name=kernel.__name__,
     )(*operands)
@@ -293,26 +297,26 @@
     )
     targets = jnp.arange(CHUNKS, dtype=i32)
     outgoing = jnp.where((targets > y)[:, None, None], own_kv[None], above_kv[None])
+    outgoing, queries = lax.optimization_barrier((outgoing, queries))
     halo = lax.all_to_all(outgoing, "y", 0, 0, tiled=True)
+    halo, gradients_weight = lax.optimization_barrier((halo, output_weight))
     out_grad = call(
-        grad_kernel, [((ROWS, Q_HEADS * HEAD), bf16)], gradients_part, output_weight
+        grad_kernel, [((ROWS, Q_HEADS * HEAD), bf16)], gradients_part, gradients_weight
     )
     probs = pltpu.VMEM((CHUNKS + 1, ROWS, ROWS), f32)
-    attended = call(
-        forward_kernel, [((ROWS, Q_HEADS * HEAD), bf16)], place, queries, halo, own_kv, scratch=[probs]
-    )
-    out_part = call(out_kernel, [((ROWS, width), bf16)], attended, output_weight)
-    out_sum = lax.psum_scatter(out_part, TP, scatter_dimension=0, tiled=True)
-    query_back, halo_back, own_back = call(
-        backward_kernel,
+    attended, query_back, halo_back, own_back = call(
+        attention_kernel,
         [
+            ((ROWS, Q_HEADS * HEAD), bf16),
             ((ROWS, Q_HEADS * HEAD), bf16),
             ((CHUNKS, ROWS, 2 * HEAD), bf16),
             ((ROWS, 2 * HEAD), f32),
         ],
-        place, queries, halo, own_kv, out_grad, attended, query_raw, query_gain, cos, sin,
+        place, queries, halo, own_kv, out_grad, query_raw, query_gain, cos, sin,
         scratch=[probs, pltpu.VMEM((CHUNKS + 1, ROWS, 2 * HEAD), f32)],
     )
+    out_part = call(out_kernel, [((ROWS, width), bf16)], attended, output_weight)
+    out_sum = lax.psum_scatter(out_part, TP, scatter_dimension=0, tiled=True)
     back = lax.all_to_all(halo_back, "y", 0, 0, tiled=True)
     own_sum, above_sum = call(
         gather_kernel,

time: 159 us -> 155 us (0.975)
  blocking collectives: 11.4 us -> 24.9 us
  starting transfers between devices: 43 us -> 33.6 us
  local copies, waits for them, and re-layouts: 12.6 us -> 8.03 us
  Pallas kernels: 17.3 us -> 14.4 us
    all_to_all x0 -> x1, blocking collectives: none -> 12.6 us  [on_device(): halo = lax.all_to_all(outgoing, 'y', 0, 0, tiled=True)]
    all_to_all x1, starting transfers between devices: 17.5 us -> 12.8 us  [on_device(): lax.all_to_all(pair.reshape(CHUNKS, PIECE, width), 'zl', 0, 0, tiled=True)]
    all_to_all x1 -> x0, starting transfers between devices: 4.65 us -> none  [on_device(): halo = lax.all_to_all(outgoing, 'y', 0, 0, tiled=True)]
    unnamed x60 -> x52, local copies, waits for them, and re-layouts: 12.6 us -> 8.03 us
    pallas_call x12 -> x11, Pallas kernels: 17.3 us -> 14.4 us  [call(): pl.pallas_call(kernel, out_shape=shapes, in_specs=in_specs, out_specs=out...]
  transfers between devices with their start and end apart: 9 -> 8, of which waited for: 7 -> 7; matrix products, arithmetic and copies ran while one was open for 2% -> 2% of each run, Pallas kernels for 10% -> 5%
where the time goes in v3:
time: 155 us; the launch traced here: 154 us
  waiting for transfers between devices  56.6 us (37%)
  starting transfers between devices  33.6 us (22%)
  blocking collectives  24.9 us (16%)
  Pallas kernels  14.4 us (9%)
  between operations  14.3 us (9%)
  local copies, waits for them, and re-layouts  8.03 us (5%)
  other arithmetic  2.51 us (2%)
    ppermute x2, waiting for transfers between devices, shift_rows(): return lax.ppermute(block, ('zh', 'x'), route)  17.6 us
    all_to_all x1, waiting for transfers between devices, on_device(): mine = lax.all_to_all(copies, 'zl', 0, 0, tiled=True).reshape(HALF, width)  17.2 us
    all_to_all x1, waiting for transfers between devices, on_device(): lax.all_to_all(pair.reshape(CHUNKS, PIECE, width), 'zl', 0, 0, tiled=True)  16.7 us
    pallas_call x11, Pallas kernels, call(): pl.pallas_call(kernel, out_shape=shapes, in_specs=in_specs, out_specs=out...  14.4 us
    all_to_all x1, starting transfers between devices, on_device(): lax.all_to_all(pair.reshape(CHUNKS, PIECE, width), 'zl', 0, 0, tiled=True)  12.8 us
    all_to_all x1, blocking collectives, on_device(): halo = lax.all_to_all(outgoing, 'y', 0, 0, tiled=True)  12.6 us
    all_to_all x1, blocking collectives, on_device(): back = lax.all_to_all(halo_back, 'y', 0, 0, tiled=True)  12.3 us
    ppermute x2, starting transfers between devices, shift_rows(): return lax.ppermute(block, ('zh', 'x'), route)  10.9 us
  transfers between devices with their start and end apart: 8, of which 7 were waited for; matrix products, arithmetic and copies ran while one was open for 2% of the time, Pallas kernels for 5%

profile of v3, /device:TPU:6, one launch (start us, length us, event | category | flops | bytes accessed | tf_op | source)
XLA Modules:
  0.0 154.3 jit_solution(3477120008387190778)
XLA Ops:
  9.0 6.0 %all-to-all-start = ((bf16[4,32,2688]{2,1,0:T(8,128)(2,1)}), bf16[4,32,2688]{2,1,0:T(8,128)(2,1)S(1)}, u32[]{:S(2)}, u32[]{:S(2)}) async-start(bf16[4,32,2688]{2,1,0:T(8,128)(2,1)} %copies_kernel.1), calls=%async_computation | async-start | bytes 1376256 | tf_op jit(solution)/shard_map/all_to_all | solution.py:285
  15.8 17.2 %all-to-all-done = bf16[4,32,2688]{2,1,0:T(8,128)(2,1)S(1)} async-done(((bf16[4,32,2688]{2,1,0:T(8,128)(2,1)}), bf16[4,32,2688]{2,1,0:T(8,128)(2,1)S(1)}, u32[]{:S(2)}, u32[]{:S(2)}) %all-to-all-start) | async-done | bytes 688160 | tf_op jit(solution)/shard_map/all_to_all | solution.py:285
  33.0 1.9 %collective-permute-start = (bf16[128,2688]{1,0:T(8,128)(2,1)S(1)}, bf16[128,2688]{1,0:T(8,128)(2,1)S(1)}, u32[]{:S(2)}, u32[]{:S(2)}) collective-permute-start(bf16[128,2688]{1,0:T(8,128)(2,1)S(1)} %bitcast.7), channel_id=1, source_target_pairs={{0,1},{1,0},{2,3},{3,2},{4,5},{5,4},{6,7},{7,6},{8,9},{9,8},{10,11... | collective-permute-start | bytes 2064392 | tf_op jit(solution)/shard_map/ppermute | solution.py:32
  35.7 1.3 collective-permute-done.other
  37.1 1.4 kv_kernel.1
  38.5 9.0 %collective-permute-start.1 = (bf16[256,256]{1,0:T(8,128)(2,1)S(1)}, bf16[256,256]{1,0:T(8,128)(2,1)S(1)}, u32[]{:S(2)}, u32[]{:S(2)}) collective-permute-start(bf16[256,256]{1,0:T(8,128)(2,1)S(1)} %get-tuple-element.16.own), channel_id=1, source_target_pairs={{0,32},{32,64},{64,96},{96,128},{128,160},{160,192},{192,224},{224... | collective-permute-start | bytes 393224 | tf_op jit(solution)/shard_map/ppermute | solution.py:38
  47.6 1.3 q_kernel.1
  48.9 3.1 %collective-permute-done.1 = bf16[256,256]{1,0:T(8,128)(2,1)S(1)} collective-permute-done((bf16[256,256]{1,0:T(8,128)(2,1)S(1)}, bf16[256,256]{1,0:T(8,128)(2,1)S(1)}, u32[]{:S(2)}, u32[]{:S(2)}) %collective-permute-start.1) | collective-permute-done | bytes 131104 | tf_op jit(solution)/shard_map/ppermute | solution.py:38
  52.1 12.6 %all_to_all.20.halo = bf16[4,256,256]{2,1,0:T(8,128)(2,1)S(1)} all-to-all(bf16[4,256,256]{2,1,0:T(8,128)(2,1)S(1)} %broadcast_select_fusion), channel_id=1, replica_groups=mesh['zh'=4,'x'=4,'y'=4,'zl'=4,'c'=2] {'y'}, dimensions={0} | all-to-all | bytes 1048576 | tf_op jit(solution)/shard_map/all_to_all | solution.py:301
  65.6 1.3 copy-done.6
  68.0 4.2 %attention_kernel.1 = (bf16[256,256]{1,0:T(8,128)(2,1)S(1)}, bf16[256,256]{1,0:T(8,128)(2,1)S(1)}, bf16[4,256,256]{2,1,0:T(8,128)(2,1)S(1)}, f32[256,256]{1,0:T(8,128)S(1)}) custom-call(s32[3]{0:T(128)S(1)} %pad_add_fusion.place, bf16[256,256]{1,0:T(8,128)(2,1)S(1)} %copy-done.23, bf16[4,256,256]{2,1,0:T(8,128)(2,1)S(1)} %all_to_all.20.halo, ...), custom_call_target="tpu_custom_call" | custom-call | bytes 2490892 | tf_op jit(solution)/shard_map/attention_kernel/pallas_call | solution.py:258
  74.9 1.1 copy-done.5
  76.1 1.0 copy-done.11
  77.1 12.3 %all_to_all.21.back = bf16[4,256,256]{2,1,0:T(8,128)(2,1)S(1)} all-to-all(bf16[4,256,256]{2,1,0:T(8,128)(2,1)S(1)} %copy-done.11), channel_id=1, replica_groups=mesh['zh'=4,'x'=4,'y'=4,'zl'=4,'c'=2] {'y'}, dimensions={0} | all-to-all | bytes 1048576 | tf_op jit(solution)/shard_map/all_to_all | solution.py:320
  89.4 0.9 copy-done.19
  91.1 1.9 %collective-permute-start.2 = (bf16[256,256]{1,0:T(8,128)(2,1)S(1)}, bf16[256,256]{1,0:T(8,128)(2,1)S(1)}, u32[]{:S(2)}, u32[]{:S(2)}) collective-permute-start(bf16[256,256]{1,0:T(8,128)(2,1)S(1)} %get-tuple-element.28), channel_id=1, source_target_pairs={{32,0},{64,32},{96,64},{128,96},{160,128},{192,160},{224,192},{256... | collective-permute-start | bytes 393224 | tf_op jit(solution)/shard_map/ppermute | solution.py:38
  93.6 14.5 %collective-permute-done.2.below = bf16[256,256]{1,0:T(8,128)(2,1)S(1)} collective-permute-done((bf16[256,256]{1,0:T(8,128)(2,1)S(1)}, bf16[256,256]{1,0:T(8,128)(2,1)S(1)}, u32[]{:S(2)}, u32[]{:S(2)}) %collective-permute-start.2) | collective-permute-done | bytes 131104 | tf_op jit(solution)/shard_map/ppermute | solution.py:38
  108.2 1.2 end_given_kernel.1
  109.4 1.9 %collective-permute-start.3 = (bf16[128,2688]{1,0:T(8,128)(2,1)S(1)}, bf16[128,2688]{1,0:T(8,128)(2,1)S(1)}, u32[]{:S(2)}, u32[]{:S(2)}) collective-permute-start(bf16[128,2688]{1,0:T(8,128)(2,1)S(1)} %end_given_kernel.1), channel_id=1, source_target_pairs={{0,1},{1,0},{2,3},{3,2},{4,5},{5,4},{6,7},{7,6},{8,9},{9,8},{10,11... | collective-permute-start | bytes 2064392 | tf_op jit(solution)/shard_map/ppermute | solution.py:32
  111.3 2.1 %collective-permute-done.3.arrived = bf16[128,2688]{1,0:T(8,128)(2,1)S(1)} collective-permute-done((bf16[128,2688]{1,0:T(8,128)(2,1)S(1)}, bf16[128,2688]{1,0:T(8,128)(2,1)S(1)}, u32[]{:S(2)}, u32[]{:S(2)}) %collective-permute-start.3) | collective-permute-done | bytes 688160 | tf_op jit(solution)/shard_map/ppermute | solution.py:32
  113.4 2.1 %end_pair_kernel.1 = bf16[128,2688]{1,0:T(8,128)(2,1)} custom-call(s32[3]{0:T(128)S(1)} %pad_add_fusion.place, f32[256,2688]{1,0:T(8,128)S(1)} %base_kernel.1.base, f32[256,256]{1,0:T(8,128)S(1)} %get-tuple-element.27.own, bf16[256,256]{1,0:T(8,128)(2,1)S(1)} %collective-permute-done.2.below, f32[256,128]{1,0:T(8,128)S(1)} %copy-done.15, ...), custom_call_target="tpu_custom_call" | custom-call | bytes 6291980 | tf_op jit(solution)/shard_map/end_pair_kernel/pallas_call | solution.py:258
  115.6 12.8 %all-to-all-start.3 = ((bf16[4,32,2688]{2,1,0:T(8,128)(2,1)}), bf16[4,32,2688]{2,1,0:T(8,128)(2,1)S(1)}, u32[]{:S(2)}, u32[]{:S(2)}) async-start(bf16[4,32,2688]{2,1,0:T(8,128)(2,1)} %bitcast.6), calls=%async_computation.4 | async-start | bytes 1376256 | tf_op jit(solution)/shard_map/all_to_all | solution.py:331
  128.4 1.6 %add_convert_fusion = bf16[32,2688]{1,0:T(8,128)(2,1)} fusion(bf16[32,2688]{1,0:T(8,128)(2,1)} %reduce-scatter.2.cloned.1.call-done, bf16[32,2688]{1,0:T(8,128)(2,1)S(1)} %copy-done.8), kind=kLoop, calls=%fused_computation.1 | loop fusion | flops 344064 | bytes 516096 | tf_op jit(solution)/shard_map/convert_element_type | solution.py:332
  130.0 16.7 %all-to-all-done.3.pieces = bf16[4,32,2688]{2,1,0:T(8,128)(2,1)S(1)} async-done(((bf16[4,32,2688]{2,1,0:T(8,128)(2,1)}), bf16[4,32,2688]{2,1,0:T(8,128)(2,1)S(1)}, u32[]{:S(2)}, u32[]{:S(2)}) %all-to-all-start.3) | async-done | bytes 688160 | tf_op jit(solution)/shard_map/all_to_all | solution.py:331
  (67 shorter events, 10.2 us)
Async XLA Ops:
  9.0 28.1 %copy-start = (bf16[2688,128]{1,0:T(8,128)(2,1)S(1)}, bf16[2688,128]{1,0:T(8,128)(2,1)}, u32[]{:S(2)}) copy-start(bf16[2688,128]{1,0:T(8,128)(2,1)} %wk.5) | copy-start | bytes 2064388
  9.0 28.1 %copy-start.1 = (bf16[2688,128]{1,0:T(8,128)(2,1)S(1)}, bf16[2688,128]{1,0:T(8,128)(2,1)}, u32[]{:S(2)}) copy-start(bf16[2688,128]{1,0:T(8,128)(2,1)} %wv.5) | copy-start | bytes 2064388
  9.0 28.1 %copy-start.24 = (f32[128]{0:T(128)S(1)}, f32[128]{0:T(128)}, u32[]{:S(2)}) copy-start(f32[128]{0:T(128)} %param.15) | copy-start | bytes 1540
  9.0 24.0 %all-to-all-start = ((bf16[4,32,2688]{2,1,0:T(8,128)(2,1)}), bf16[4,32,2688]{2,1,0:T(8,128)(2,1)S(1)}, u32[]{:S(2)}, u32[]{:S(2)}) async-start(bf16[4,32,2688]{2,1,0:T(8,128)(2,1)} %copies_kernel.1), calls=%async_computation | async-start | bytes 1376256 | tf_op jit(solution)/shard_map/all_to_all | solution.py:285
  15.0 50.6 %all-gather.2.cloned.1.call-start = ((), (), s32[]{:S(2)}) async-start(), calls=%async_computation.5 | async-start | bytes 1548288 | tf_op jit(solution)/shard_map/all_gather | solution.py:283
  15.7 112.6 %reduce-scatter.2.cloned.1.call-start = ((), (), s32[]{:S(2)}) async-start(), calls=%async_computation.6 | async-start | bytes 1548288 | tf_op jit(solution)/shard_map/reduce_scatter | solution.py:319
  33.0 4.0 %collective-permute-start = (bf16[128,2688]{1,0:T(8,128)(2,1)S(1)}, bf16[128,2688]{1,0:T(8,128)(2,1)S(1)}, u32[]{:S(2)}, u32[]{:S(2)}) collective-permute-start(bf16[128,2688]{1,0:T(8,128)(2,1)S(1)} %bitcast.7), channel_id=1, source_target_pairs={{0,1},{1,0},{2,3},{3,2},{4,5},{5,4},{6,7},{7,6},{8,9},{9,8},{10,11... | collective-permute-start | bytes 2064392 | tf_op jit(solution)/shard_map/ppermute | solution.py:32
  37.1 10.5 %copy-start.3 = (bf16[2688,256]{1,0:T(8,128)(2,1)S(1)}, bf16[2688,256]{1,0:T(8,128)(2,1)}, u32[]{:S(2)}) copy-start(bf16[2688,256]{1,0:T(8,128)(2,1)} %wq.3) | copy-start | bytes 4128772
  37.1 10.5 %copy-start.25 = (f32[128]{0:T(128)S(1)}, f32[128]{0:T(128)}, u32[]{:S(2)}) copy-start(f32[128]{0:T(128)} %param.14) | copy-start | bytes 1540
  38.5 10.4 %copy-start.14 = (f32[256,128]{1,0:T(8,128)}, f32[256,128]{1,0:T(8,128)S(1)}, u32[]{:S(2)}) copy-start(f32[256,128]{1,0:T(8,128)S(1)} %get-tuple-element.29.k_raw) | copy-start | bytes 393220
  38.5 13.5 %copy-start.12 = (bf16[256,256]{1,0:T(8,128)(2,1)}, bf16[256,256]{1,0:T(8,128)(2,1)S(1)}, u32[]{:S(2)}) copy-start(bf16[256,256]{1,0:T(8,128)(2,1)S(1)} %get-tuple-element.16.own) | copy-start | bytes 393220
  38.5 13.5 %collective-permute-start.1 = (bf16[256,256]{1,0:T(8,128)(2,1)S(1)}, bf16[256,256]{1,0:T(8,128)(2,1)S(1)}, u32[]{:S(2)}, u32[]{:S(2)}) collective-permute-start(bf16[256,256]{1,0:T(8,128)(2,1)S(1)} %get-tuple-element.16.own), channel_id=1, source_target_pairs={{0,32},{32,64},{64,96},{96,128},{128,160},{160,192},{192,224},{224... | collective-permute-start | bytes 393224 | tf_op jit(solution)/shard_map/ppermute | solution.py:38
  48.9 3.2 %copy-start.16 = (f32[256,256]{1,0:T(8,128)}, f32[256,256]{1,0:T(8,128)S(1)}, u32[]{:S(2)}) copy-start(f32[256,256]{1,0:T(8,128)S(1)} %get-tuple-element.22.q_raw) | copy-start | bytes 786436
  48.9 3.2 %copy-start.22 = (bf16[256,256]{1,0:T(8,128)(2,1)}, bf16[256,256]{1,0:T(8,128)(2,1)S(1)}, u32[]{:S(2)}) copy-start(bf16[256,256]{1,0:T(8,128)(2,1)S(1)} %get-tuple-element.18.q) | copy-start | bytes 393220
  48.9 16.7 %copy-start.2 = (bf16[256,2688]{1,0:T(8,128)(2,1)S(1)}, bf16[256,2688]{1,0:T(8,128)(2,1)}, u32[]{:S(2)}) copy-start(bf16[256,2688]{1,0:T(8,128)(2,1)} %wo.2) | copy-start | bytes 4128772
  65.6 1.3 copy-start.6
  76.0 17.0 %copy-start.4 = (bf16[2688,256]{1,0:T(8,128)(2,1)S(1)}, bf16[2688,256]{1,0:T(8,128)(2,1)}, u32[]{:S(2)}) copy-start(bf16[2688,256]{1,0:T(8,128)(2,1)} %wq.3) | copy-start | bytes 4128772
  76.1 17.0 %copy-start.21 = (bf16[256,256]{1,0:T(8,128)(2,1)S(1)}, bf16[256,256]{1,0:T(8,128)(2,1)}, u32[]{:S(2)}) copy-start(bf16[256,256]{1,0:T(8,128)(2,1)} %copy-done.20) | copy-start | bytes 393220
  91.1 17.1 %collective-permute-start.2 = (bf16[256,256]{1,0:T(8,128)(2,1)S(1)}, bf16[256,256]{1,0:T(8,128)(2,1)S(1)}, u32[]{:S(2)}, u32[]{:S(2)}) collective-permute-start(bf16[256,256]{1,0:T(8,128)(2,1)S(1)} %get-tuple-element.28), channel_id=1, source_target_pairs={{32,0},{64,32},{96,64},{128,96},{160,128},{192,160},{224,192},{256... | collective-permute-start | bytes 393224 | tf_op jit(solution)/shard_map/ppermute | solution.py:38
  93.1 15.1 %copy-start.15 = (f32[256,128]{1,0:T(8,128)S(1)}, f32[256,128]{1,0:T(8,128)}, u32[]{:S(2)}) copy-start(f32[256,128]{1,0:T(8,128)} %copy-done.14) | copy-start | bytes 393220
  109.4 4.0 %collective-permute-start.3 = (bf16[128,2688]{1,0:T(8,128)(2,1)S(1)}, bf16[128,2688]{1,0:T(8,128)(2,1)S(1)}, u32[]{:S(2)}, u32[]{:S(2)}) collective-permute-start(bf16[128,2688]{1,0:T(8,128)(2,1)S(1)} %end_given_kernel.1), channel_id=1, source_target_pairs={{0,1},{1,0},{2,3},{3,2},{4,5},{5,4},{6,7},{7,6},{8,9},{9,8},{10,11... | collective-permute-start | bytes 2064392 | tf_op jit(solution)/shard_map/ppermute | solution.py:32
  115.6 12.8 %copy-start.8 = (bf16[32,2688]{1,0:T(8,128)(2,1)S(1)}, bf16[32,2688]{1,0:T(8,128)(2,1)}, u32[]{:S(2)}) copy-start(bf16[32,2688]{1,0:T(8,128)(2,1)} %tokens_ref.1) | copy-start | bytes 516100
  115.6 31.1 %copy-start.9 = (bf16[32,2688]{1,0:T(8,128)(2,1)S(1)}, bf16[32,2688]{1,0:T(8,128)(2,1)}, u32[]{:S(2)}) copy-start(bf16[32,2688]{1,0:T(8,128)(2,1)} %first.1) | copy-start | bytes 516100
  115.6 31.1 %all-to-all-start.3 = ((bf16[4,32,2688]{2,1,0:T(8,128)(2,1)}), bf16[4,32,2688]{2,1,0:T(8,128)(2,1)S(1)}, u32[]{:S(2)}, u32[]{:S(2)}) async-start(bf16[4,32,2688]{2,1,0:T(8,128)(2,1)} %bitcast.6), calls=%async_computation.4 | async-start | bytes 1376256 | tf_op jit(solution)/shard_map/all_to_all | solution.py:331
  (10 other events, 9.2 us)
Sparse Core Ops, SparseCore 0:
  17.9 47.6 all-gather.1
  76.2 51.3 reduce-scatter.1

commit v4 on v3

--- a/solution.py
+++ b/solution.py
@@ -1,4 +1,4 @@
-import functools
+import math
 
 import jax
 import jax.numpy as jnp
@@ -143,9 +143,10 @@
 
 
 def attention_kernel(
-    place, q, halo, own, grad, q_raw, gain, cos, sin,
-    attended_out, q_back, halo_back, own_back, probs, dkv,
+    place, q, halo, own, grad_rows, wo, q_raw, gain, cos, sin,
+    out_part, q_back, halo_back, own_back, probs, dkv, grad, attended_out,
 ):
+    grad_kernel(grad_rows, wo, grad)
     allowed = masks(place, 0)
     for h in range(Q_HEADS):
         cols = slice(h * HEAD, (h + 1) * HEAD)
@@ -193,6 +194,7 @@
         q_back[:, cols] = norm_rope_back(
             q_raw[:, cols], gain[...], cos[...], sin[...], jnp.transpose(query_grad)
         ).astype(bf16)
+    out_kernel(attended_out, wo, out_part)
 
 
 def gather_kernel(place, back, own_back, own_out, above_out):
@@ -244,7 +246,10 @@
     in_specs = [
         pl.BlockSpec(memory_space=pltpu.SMEM if a.dtype == i32 else pltpu.VMEM) for a in operands
     ]
-    shapes = [jax.ShapeDtypeStruct(shape, dtype) for shape, dtype in outs]
+    shapes = [
+        pltpu.HBM(shape, dtype) if kept else jax.ShapeDtypeStruct(shape, dtype)
+        for shape, dtype, kept in ((*out, False)[:3] for out in outs)
+    ]
     out_specs = [pl.BlockSpec(memory_space=pltpu.VMEM)] * len(shapes)
     grid = ()
     if BLOCKED:
@@ -254,7 +259,7 @@
         ]
         out_specs = [whole(a) for a in shapes]
         grid = (1,)
-    size = sum(a.size * a.dtype.itemsize for a in (*operands, *shapes))
+    size = sum(math.prod(a.shape) * a.dtype.itemsize for a in (*operands, *shapes))
     results = pl.pallas_call(
         kernel,
         out_shape=shapes,
@@ -286,13 +291,13 @@
     other = swap_cores(mine)
     own_kv, key_raw = call(
         kv_kernel,
-        [((ROWS, 2 * HEAD), bf16), ((ROWS, HEAD), f32)],
+        [((ROWS, 2 * HEAD), bf16), ((ROWS, HEAD), f32, True)],
         place, mine, other, key_weight, value_weight, key_gain, cos, sin,
     )
     above_kv = shift_rows(own_kv, 1)
     queries, query_raw = call(
         q_kernel,
-        [((ROWS, Q_HEADS * HEAD), bf16), ((ROWS, Q_HEADS * HEAD), f32)],
+        [((ROWS, Q_HEADS * HEAD), bf16, True), ((ROWS, Q_HEADS * HEAD), f32, True)],
         place, mine, other, query_weight, query_gain, cos, sin,
     )
     targets = jnp.arange(CHUNKS, dtype=i32)
@@ -300,28 +305,31 @@
     outgoing, queries = lax.optimization_barrier((outgoing, queries))
     halo = lax.all_to_all(outgoing, "y", 0, 0, tiled=True)
     halo, gradients_weight = lax.optimization_barrier((halo, output_weight))
-    out_grad = call(
-        grad_kernel, [((ROWS, Q_HEADS * HEAD), bf16)], gradients_part, gradients_weight
-    )
     probs = pltpu.VMEM((CHUNKS + 1, ROWS, ROWS), f32)
-    attended, query_back, halo_back, own_back = call(
+    in_hbm = lambda a: pltpu.with_memory_space_constraint(a, pltpu.HBM)
+    out_part, query_back, halo_back, own_back = call(
         attention_kernel,
         [
-            ((ROWS, Q_HEADS * HEAD), bf16),
-            ((ROWS, Q_HEADS * HEAD), bf16),
+            ((ROWS, width), bf16, True),
+            ((ROWS, Q_HEADS * HEAD), bf16, True),
             ((CHUNKS, ROWS, 2 * HEAD), bf16),
-            ((ROWS, 2 * HEAD), f32),
+            ((ROWS, 2 * HEAD), f32, True),
         ],
-        place, queries, halo, own_kv, out_grad, query_raw, query_gain, cos, sin,
-        scratch=[probs, pltpu.VMEM((CHUNKS + 1, ROWS, 2 * HEAD), f32)],
-    )
-    out_part = call(out_kernel, [((ROWS, width), bf16)], attended, output_weight)
+        place, in_hbm(queries), halo, in_hbm(own_kv), in_hbm(gradients_part), in_hbm(gradients_weight),
+        in_hbm(query_raw), query_gain, in_hbm(cos), in_hbm(sin),
+        scratch=[
+            probs,
+            pltpu.VMEM((CHUNKS + 1, ROWS, 2 * HEAD), f32),
+            pltpu.VMEM((ROWS, Q_HEADS * HEAD), bf16),
+            pltpu.VMEM((ROWS, Q_HEADS * HEAD), bf16),
+        ],
+    )
     out_sum = lax.psum_scatter(out_part, TP, scatter_dimension=0, tiled=True)
     back = lax.all_to_all(halo_back, "y", 0, 0, tiled=True)
     own_sum, above_sum = call(
         gather_kernel,
         [((ROWS, 2 * HEAD), f32), ((ROWS, 2 * HEAD), bf16)],
-        place, back, own_back,
+        place, back, in_hbm(own_back),
     )
     below = shift_rows(above_sum, -1)
     base = call(base_kernel, [((ROWS, width), f32)], query_back, query_weight)

time: 155 us -> 153 us (0.987)
  local copies, waits for them, and re-layouts: 8.03 us -> 2.8 us
  waiting for transfers between devices: 56.6 us -> 51.7 us
  starting transfers between devices: 33.6 us -> 38.1 us
  Pallas kernels: 14.4 us -> 18.2 us
    unnamed x52 -> x34, local copies, waits for them, and re-layouts: 8.03 us -> 2.8 us
    all_to_all x1, starting transfers between devices: 12.8 us -> 17.3 us  [on_device(): lax.all_to_all(pair.reshape(CHUNKS, PIECE, width), 'zl', 0, 0, tiled=True)]
    ppermute x2, waiting for transfers between devices: 17.6 us -> 13.6 us  [shift_rows(): return lax.ppermute(block, ('zh', 'x'), route)]
    pallas_call x11 -> x9, Pallas kernels: 14.4 us -> 18.2 us  [call(): pl.pallas_call(kernel, out_shape=shapes, in_specs=in_specs, out_specs=out...]
  transfers between devices with their start and end apart: 8 -> 8, of which waited for: 7 -> 6; matrix products, arithmetic and copies ran while one was open for 2% -> 2% of each run, Pallas kernels for 5% -> 6%
where the time goes in v4:
time: 153 us; the launch traced here: 152 us
  waiting for transfers between devices  51.7 us (34%)
  starting transfers between devices  38.1 us (25%)
  blocking collectives  24.7 us (16%)
  Pallas kernels  18.2 us (12%)
  between operations  14.2 us (9%)
  local copies, waits for them, and re-layouts  2.8 us (2%)
  other arithmetic  2.52 us (2%)
    pallas_call x9, Pallas kernels, call(): pl.pallas_call(kernel, out_shape=shapes, in_specs=in_specs, out_specs=out...  18.2 us
    all_to_all x1, starting transfers between devices, on_device(): lax.all_to_all(pair.reshape(CHUNKS, PIECE, width), 'zl', 0, 0, tiled=True)  17.3 us
    all_to_all x1, waiting for transfers between devices, on_device(): mine = lax.all_to_all(copies, 'zl', 0, 0, tiled=True).reshape(HALF, width)  17.2 us
    all_to_all x1, waiting for transfers between devices, on_device(): lax.all_to_all(pair.reshape(CHUNKS, PIECE, width), 'zl', 0, 0, tiled=True)  16.7 us
    ppermute x2, waiting for transfers between devices, shift_rows(): return lax.ppermute(block, ('zh', 'x'), route)  13.6 us
    all_to_all x1, blocking collectives, on_device(): halo = lax.all_to_all(outgoing, 'y', 0, 0, tiled=True)  12.5 us
    all_to_all x1, blocking collectives, on_device(): back = lax.all_to_all(halo_back, 'y', 0, 0, tiled=True)  12.2 us
    ppermute x2, starting transfers between devices, shift_rows(): return lax.ppermute(block, ('zh', 'x'), route)  10.9 us
  transfers between devices with their start and end apart: 8, of which 6 were waited for; matrix products, arithmetic and copies ran while one was open for 2% of the time, Pallas kernels for 6%

profile of v4, /device:TPU:6, one launch (start us, length us, event | category | flops | bytes accessed | tf_op | source)
XLA Modules:
  0.0 152.2 jit_solution(1301331580095054394)
XLA Ops:
  7.2 0.9 copy-done.7
  8.1 0.9 copies_kernel.1
  9.0 6.0 %all-to-all-start = ((bf16[4,32,2688]{2,1,0:T(8,128)(2,1)}), bf16[4,32,2688]{2,1,0:T(8,128)(2,1)S(1)}, u32[]{:S(2)}, u32[]{:S(2)}) async-start(bf16[4,32,2688]{2,1,0:T(8,128)(2,1)} %copies_kernel.1), calls=%async_computation | async-start | bytes 1376256 | tf_op jit(solution)/shard_map/all_to_all | solution.py:290
  15.8 17.2 %all-to-all-done = bf16[4,32,2688]{2,1,0:T(8,128)(2,1)S(1)} async-done(((bf16[4,32,2688]{2,1,0:T(8,128)(2,1)}), bf16[4,32,2688]{2,1,0:T(8,128)(2,1)S(1)}, u32[]{:S(2)}, u32[]{:S(2)}) %all-to-all-start) | async-done | bytes 688160 | tf_op jit(solution)/shard_map/all_to_all | solution.py:290
  33.0 1.9 %collective-permute-start = (bf16[128,2688]{1,0:T(8,128)(2,1)S(1)}, bf16[128,2688]{1,0:T(8,128)(2,1)S(1)}, u32[]{:S(2)}, u32[]{:S(2)}) collective-permute-start(bf16[128,2688]{1,0:T(8,128)(2,1)S(1)} %bitcast.7), channel_id=1, source_target_pairs={{0,1},{1,0},{2,3},{3,2},{4,5},{5,4},{6,7},{7,6},{8,9},{9,8},{10,11... | collective-permute-start | bytes 2064392 | tf_op jit(solution)/shard_map/ppermute | solution.py:32
  35.8 1.3 collective-permute-done.other
  37.1 2.1 %kv_kernel.1 = (bf16[256,256]{1,0:T(8,128)(2,1)S(1)}, f32[256,128]{1,0:T(8,128)}) custom-call(s32[3]{0:T(128)S(1)} %pad_add_fusion.place, bf16[128,2688]{1,0:T(8,128)(2,1)S(1)} %bitcast.8, bf16[128,2688]{1,0:T(8,128)(2,1)S(1)} %collective-permute-done.other, bf16[2688,128]{1,0:T(8,128)(2,1)S(1)} %copy-done, bf16[2688,128]{1,0:T(8,128)(2,1)S(1)} %copy-done.1, ...), custom_call_target="tpu_custom_call" | custom-call | bytes 3277324 | tf_op jit(solution)/shard_map/kv_kernel/pallas_call | solution.py:263
  39.2 9.0 %collective-permute-start.1 = (bf16[256,256]{1,0:T(8,128)(2,1)S(1)}, bf16[256,256]{1,0:T(8,128)(2,1)S(1)}, u32[]{:S(2)}, u32[]{:S(2)}) collective-permute-start(bf16[256,256]{1,0:T(8,128)(2,1)S(1)} %get-tuple-element.16.own), channel_id=1, source_target_pairs={{0,32},{32,64},{64,96},{96,128},{128,160},{160,192},{192,224},{224... | collective-permute-start | bytes 393224 | tf_op jit(solution)/shard_map/ppermute | solution.py:38
  48.2 2.0 %q_kernel.1 = (bf16[256,256]{1,0:T(8,128)(2,1)}, f32[256,256]{1,0:T(8,128)}) custom-call(s32[3]{0:T(128)S(1)} %pad_add_fusion.place, bf16[128,2688]{1,0:T(8,128)(2,1)S(1)} %bitcast.9, bf16[128,2688]{1,0:T(8,128)(2,1)S(1)} %collective-permute-done.other, bf16[2688,256]{1,0:T(8,128)(2,1)S(1)} %copy-done.2, f32[1,128]{1,0:T(1,128)S(1)} %bitcast.13, ...), custom_call_target="tpu_custom_call" | custom-call | bytes 3408396 | tf_op jit(solution)/shard_map/q_kernel/pallas_call | solution.py:263
  50.2 3.2 %collective-permute-done.1 = bf16[256,256]{1,0:T(8,128)(2,1)S(1)} collective-permute-done((bf16[256,256]{1,0:T(8,128)(2,1)S(1)}, bf16[256,256]{1,0:T(8,128)(2,1)S(1)}, u32[]{:S(2)}, u32[]{:S(2)}) %collective-permute-start.1) | collective-permute-done | bytes 131104 | tf_op jit(solution)/shard_map/ppermute | solution.py:38
  53.5 12.5 %all_to_all.20.halo = bf16[4,256,256]{2,1,0:T(8,128)(2,1)S(1)} all-to-all(bf16[4,256,256]{2,1,0:T(8,128)(2,1)S(1)} %broadcast_select_fusion), channel_id=1, replica_groups=mesh['zh'=4,'x'=4,'y'=4,'zl'=4,'c'=2] {'y'}, dimensions={0} | all-to-all | bytes 1048576 | tf_op jit(solution)/shard_map/all_to_all | solution.py:306
  66.1 7.4 %attention_kernel.1 = (bf16[256,2688]{1,0:T(8,128)(2,1)}, bf16[256,256]{1,0:T(8,128)(2,1)}, bf16[4,256,256]{2,1,0:T(8,128)(2,1)S(1)}, f32[256,256]{1,0:T(8,128)}) custom-call(s32[3]{0:T(128)S(1)} %pad_add_fusion.place, bf16[256,256]{1,0:T(8,128)(2,1)} %get-tuple-element.18.q, bf16[4,256,256]{2,1,0:T(8,128)(2,1)S(1)} %all_to_all.20.halo, ...), custom_call_target="tpu_custom_call" | custom-call | bytes 6357516 | tf_op jit(solution)/shard_map/attention_kernel/pallas_call | solution.py:263
  74.3 1.0 copy-done.11
  75.3 12.2 %all_to_all.21.back = bf16[4,256,256]{2,1,0:T(8,128)(2,1)S(1)} all-to-all(bf16[4,256,256]{2,1,0:T(8,128)(2,1)S(1)} %copy-done.11), channel_id=1, replica_groups=mesh['zh'=4,'x'=4,'y'=4,'zl'=4,'c'=2] {'y'}, dimensions={0} | all-to-all | bytes 1048576 | tf_op jit(solution)/shard_map/all_to_all | solution.py:328
  87.4 1.2 gather_kernel.1
  88.6 1.9 %collective-permute-start.2 = (bf16[256,256]{1,0:T(8,128)(2,1)S(1)}, bf16[256,256]{1,0:T(8,128)(2,1)S(1)}, u32[]{:S(2)}, u32[]{:S(2)}) collective-permute-start(bf16[256,256]{1,0:T(8,128)(2,1)S(1)} %get-tuple-element.28), channel_id=1, source_target_pairs={{32,0},{64,32},{96,64},{128,96},{160,128},{192,160},{224,192},{256... | collective-permute-start | bytes 393224 | tf_op jit(solution)/shard_map/ppermute | solution.py:38
  91.2 10.4 %collective-permute-done.2.below = bf16[256,256]{1,0:T(8,128)(2,1)S(1)} collective-permute-done((bf16[256,256]{1,0:T(8,128)(2,1)S(1)}, bf16[256,256]{1,0:T(8,128)(2,1)S(1)}, u32[]{:S(2)}, u32[]{:S(2)}) %collective-permute-start.2) | collective-permute-done | bytes 131104 | tf_op jit(solution)/shard_map/ppermute | solution.py:38
  101.6 1.2 end_given_kernel.1
  102.9 1.9 %collective-permute-start.3 = (bf16[128,2688]{1,0:T(8,128)(2,1)S(1)}, bf16[128,2688]{1,0:T(8,128)(2,1)S(1)}, u32[]{:S(2)}, u32[]{:S(2)}) collective-permute-start(bf16[128,2688]{1,0:T(8,128)(2,1)S(1)} %end_given_kernel.1), channel_id=1, source_target_pairs={{0,1},{1,0},{2,3},{3,2},{4,5},{5,4},{6,7},{7,6},{8,9},{9,8},{10,11... | collective-permute-start | bytes 2064392 | tf_op jit(solution)/shard_map/ppermute | solution.py:32
  104.8 2.1 %collective-permute-done.3.arrived = bf16[128,2688]{1,0:T(8,128)(2,1)S(1)} collective-permute-done((bf16[128,2688]{1,0:T(8,128)(2,1)S(1)}, bf16[128,2688]{1,0:T(8,128)(2,1)S(1)}, u32[]{:S(2)}, u32[]{:S(2)}) %collective-permute-start.3) | collective-permute-done | bytes 688160 | tf_op jit(solution)/shard_map/ppermute | solution.py:32
  106.9 2.1 %end_pair_kernel.1 = bf16[128,2688]{1,0:T(8,128)(2,1)} custom-call(s32[3]{0:T(128)S(1)} %pad_add_fusion.place, f32[256,2688]{1,0:T(8,128)S(1)} %base_kernel.1.base, f32[256,256]{1,0:T(8,128)S(1)} %get-tuple-element.27.own, bf16[256,256]{1,0:T(8,128)(2,1)S(1)} %collective-permute-done.2.below, f32[256,128]{1,0:T(8,128)S(1)} %copy-done.13, ...), custom_call_target="tpu_custom_call" | custom-call | bytes 6291980 | tf_op jit(solution)/shard_map/end_pair_kernel/pallas_call | solution.py:263
  109.0 17.3 %all-to-all-start.3 = ((bf16[4,32,2688]{2,1,0:T(8,128)(2,1)}), bf16[4,32,2688]{2,1,0:T(8,128)(2,1)S(1)}, u32[]{:S(2)}, u32[]{:S(2)}) async-start(bf16[4,32,2688]{2,1,0:T(8,128)(2,1)} %bitcast.6), calls=%async_computation.4 | async-start | bytes 1376256 | tf_op jit(solution)/shard_map/all_to_all | solution.py:339
  126.3 1.6 %add_convert_fusion = bf16[32,2688]{1,0:T(8,128)(2,1)} fusion(bf16[32,2688]{1,0:T(8,128)(2,1)} %reduce-scatter.2.cloned.1.call-done, bf16[32,2688]{1,0:T(8,128)(2,1)S(1)} %copy-done.8), kind=kLoop, calls=%fused_computation.1 | loop fusion | flops 344064 | bytes 516096 | tf_op jit(solution)/shard_map/convert_element_type | solution.py:340
  127.9 16.7 %all-to-all-done.3.pieces = bf16[4,32,2688]{2,1,0:T(8,128)(2,1)S(1)} async-done(((bf16[4,32,2688]{2,1,0:T(8,128)(2,1)}), bf16[4,32,2688]{2,1,0:T(8,128)(2,1)S(1)}, u32[]{:S(2)}, u32[]{:S(2)}) %all-to-all-start.3) | async-done | bytes 688160 | tf_op jit(solution)/shard_map/all_to_all | solution.py:339
  (47 shorter events, 3.9 us)
Async XLA Ops:
  7.2 0.9 copy-start.7
  9.0 28.1 %copy-start = (bf16[2688,128]{1,0:T(8,128)(2,1)S(1)}, bf16[2688,128]{1,0:T(8,128)(2,1)}, u32[]{:S(2)}) copy-start(bf16[2688,128]{1,0:T(8,128)(2,1)} %wk.5) | copy-start | bytes 2064388
  9.0 28.1 %copy-start.1 = (bf16[2688,128]{1,0:T(8,128)(2,1)S(1)}, bf16[2688,128]{1,0:T(8,128)(2,1)}, u32[]{:S(2)}) copy-start(bf16[2688,128]{1,0:T(8,128)(2,1)} %wv.5) | copy-start | bytes 2064388
  9.0 28.1 %copy-start.15 = (f32[128]{0:T(128)S(1)}, f32[128]{0:T(128)}, u32[]{:S(2)}) copy-start(f32[128]{0:T(128)} %param.15) | copy-start | bytes 1540
  9.0 24.0 %all-to-all-start = ((bf16[4,32,2688]{2,1,0:T(8,128)(2,1)}), bf16[4,32,2688]{2,1,0:T(8,128)(2,1)S(1)}, u32[]{:S(2)}, u32[]{:S(2)}) async-start(bf16[4,32,2688]{2,1,0:T(8,128)(2,1)} %copies_kernel.1), calls=%async_computation | async-start | bytes 1376256 | tf_op jit(solution)/shard_map/all_to_all | solution.py:290
  15.0 51.0 %all-gather.2.cloned.1.call-start = ((), (), s32[]{:S(2)}) async-start(), calls=%async_computation.5 | async-start | bytes 1548288 | tf_op jit(solution)/shard_map/all_gather | solution.py:288
  15.8 110.5 %reduce-scatter.2.cloned.1.call-start = ((), (), s32[]{:S(2)}) async-start(), calls=%async_computation.6 | async-start | bytes 1548288 | tf_op jit(solution)/shard_map/reduce_scatter | solution.py:327
  33.0 4.0 %collective-permute-start = (bf16[128,2688]{1,0:T(8,128)(2,1)S(1)}, bf16[128,2688]{1,0:T(8,128)(2,1)S(1)}, u32[]{:S(2)}, u32[]{:S(2)}) collective-permute-start(bf16[128,2688]{1,0:T(8,128)(2,1)S(1)} %bitcast.7), channel_id=1, source_target_pairs={{0,1},{1,0},{2,3},{3,2},{4,5},{5,4},{6,7},{7,6},{8,9},{9,8},{10,11... | collective-permute-start | bytes 2064392 | tf_op jit(solution)/shard_map/ppermute | solution.py:32
  35.7 12.5 %copy-start.3 = (f32[256,128]{1,0:T(8,128)}, f32[256,128]{1,0:T(8,128)S(1)}, u32[]{:S(2)}) copy-start(f32[256,128]{1,0:T(8,128)S(1)} %get-tuple-element.33.cos) | copy-start | bytes 393220
  35.7 12.5 %copy-start.5 = (f32[256,128]{1,0:T(8,128)}, f32[256,128]{1,0:T(8,128)S(1)}, u32[]{:S(2)}) copy-start(f32[256,128]{1,0:T(8,128)S(1)} %get-tuple-element.34.sin) | copy-start | bytes 393220
  37.1 11.1 %copy-start.2 = (bf16[2688,256]{1,0:T(8,128)(2,1)S(1)}, bf16[2688,256]{1,0:T(8,128)(2,1)}, u32[]{:S(2)}) copy-start(bf16[2688,256]{1,0:T(8,128)(2,1)} %wq.3) | copy-start | bytes 4128772
  37.1 11.1 %copy-start.16 = (f32[128]{0:T(128)S(1)}, f32[128]{0:T(128)}, u32[]{:S(2)}) copy-start(f32[128]{0:T(128)} %param.14) | copy-start | bytes 1540
  39.2 14.2 %copy-start.12 = (bf16[256,256]{1,0:T(8,128)(2,1)}, bf16[256,256]{1,0:T(8,128)(2,1)S(1)}, u32[]{:S(2)}) copy-start(bf16[256,256]{1,0:T(8,128)(2,1)S(1)} %get-tuple-element.16.own) | copy-start | bytes 393220
  39.2 14.2 %collective-permute-start.1 = (bf16[256,256]{1,0:T(8,128)(2,1)S(1)}, bf16[256,256]{1,0:T(8,128)(2,1)S(1)}, u32[]{:S(2)}, u32[]{:S(2)}) collective-permute-start(bf16[256,256]{1,0:T(8,128)(2,1)S(1)} %get-tuple-element.16.own), channel_id=1, source_target_pairs={{0,32},{32,64},{64,96},{96,128},{128,160},{160,192},{192,224},{224... | collective-permute-start | bytes 393224 | tf_op jit(solution)/shard_map/ppermute | solution.py:38
  74.2 1.0 copy-start.11
  74.2 16.3 %copy-start.14 = (bf16[256,256]{1,0:T(8,128)(2,1)S(1)}, bf16[256,256]{1,0:T(8,128)(2,1)}, u32[]{:S(2)}) copy-start(bf16[256,256]{1,0:T(8,128)(2,1)} %get-tuple-element.24.q_back) | copy-start | bytes 393220
  88.6 13.0 %collective-permute-start.2 = (bf16[256,256]{1,0:T(8,128)(2,1)S(1)}, bf16[256,256]{1,0:T(8,128)(2,1)S(1)}, u32[]{:S(2)}, u32[]{:S(2)}) collective-permute-start(bf16[256,256]{1,0:T(8,128)(2,1)S(1)} %get-tuple-element.28), channel_id=1, source_target_pairs={{32,0},{64,32},{96,64},{128,96},{160,128},{192,160},{224,192},{256... | collective-permute-start | bytes 393224 | tf_op jit(solution)/shard_map/ppermute | solution.py:38
  90.6 11.0 %copy-start.4 = (f32[256,128]{1,0:T(8,128)S(1)}, f32[256,128]{1,0:T(8,128)}, u32[]{:S(2)}) copy-start(f32[256,128]{1,0:T(8,128)} %copy-done.3) | copy-start | bytes 393220
  90.6 11.0 %copy-start.6 = (f32[256,128]{1,0:T(8,128)S(1)}, f32[256,128]{1,0:T(8,128)}, u32[]{:S(2)}) copy-start(f32[256,128]{1,0:T(8,128)} %copy-done.5) | copy-start | bytes 393220
  90.6 11.0 %copy-start.13 = (f32[256,128]{1,0:T(8,128)S(1)}, f32[256,128]{1,0:T(8,128)}, u32[]{:S(2)}) copy-start(f32[256,128]{1,0:T(8,128)} %get-tuple-element.29.k_raw) | copy-start | bytes 393220
  102.9 4.0 %collective-permute-start.3 = (bf16[128,2688]{1,0:T(8,128)(2,1)S(1)}, bf16[128,2688]{1,0:T(8,128)(2,1)S(1)}, u32[]{:S(2)}, u32[]{:S(2)}) collective-permute-start(bf16[128,2688]{1,0:T(8,128)(2,1)S(1)} %end_given_kernel.1), channel_id=1, source_target_pairs={{0,1},{1,0},{2,3},{3,2},{4,5},{5,4},{6,7},{7,6},{8,9},{9,8},{10,11... | collective-permute-start | bytes 2064392 | tf_op jit(solution)/shard_map/ppermute | solution.py:32
  109.0 17.3 %copy-start.8 = (bf16[32,2688]{1,0:T(8,128)(2,1)S(1)}, bf16[32,2688]{1,0:T(8,128)(2,1)}, u32[]{:S(2)}) copy-start(bf16[32,2688]{1,0:T(8,128)(2,1)} %tokens_ref.1) | copy-start | bytes 516100
  109.0 35.6 %copy-start.9 = (bf16[32,2688]{1,0:T(8,128)(2,1)S(1)}, bf16[32,2688]{1,0:T(8,128)(2,1)}, u32[]{:S(2)}) copy-start(bf16[32,2688]{1,0:T(8,128)(2,1)} %first.1) | copy-start | bytes 516100
  109.0 35.6 %all-to-all-start.3 = ((bf16[4,32,2688]{2,1,0:T(8,128)(2,1)}), bf16[4,32,2688]{2,1,0:T(8,128)(2,1)S(1)}, u32[]{:S(2)}, u32[]{:S(2)}) async-start(bf16[4,32,2688]{2,1,0:T(8,128)(2,1)} %bitcast.6), calls=%async_computation.4 | async-start | bytes 1376256 | tf_op jit(solution)/shard_map/all_to_all | solution.py:339
  (1 other events, 0.8 us)
Sparse Core Ops, SparseCore 0:
  17.9 48.0 all-gather.1
  74.4 51.5 reduce-scatter.1

commit v5 on v4

--- a/solution.py
+++ b/solution.py
@@ -286,7 +286,8 @@
     cos, sin = rope_tables(positions)
 
     gradients_part = lax.all_gather(result_grad, TP, axis=0, tiled=True)
-    copies = call(copies_kernel, [((CHUNKS, PIECE, width), bf16)], tokens)
+    in_hbm = lambda a: pltpu.with_memory_space_constraint(a, pltpu.HBM)
+    copies = call(copies_kernel, [((CHUNKS, PIECE, width), bf16, True)], in_hbm(tokens))
     mine = lax.all_to_all(copies, "zl", 0, 0, tiled=True).reshape(HALF, width)
     other = swap_cores(mine)
     own_kv, key_raw = call(
@@ -306,7 +307,6 @@
     halo = lax.all_to_all(outgoing, "y", 0, 0, tiled=True)
     halo, gradients_weight = lax.optimization_barrier((halo, output_weight))
     probs = pltpu.VMEM((CHUNKS + 1, ROWS, ROWS), f32)
-    in_hbm = lambda a: pltpu.with_memory_space_constraint(a, pltpu.HBM)
     out_part, query_back, halo_back, own_back = call(
         attention_kernel,
         [

time: 153 us -> 153 us (level)
  no operation moved by 1% of the time
where the time goes in v5:
time: 153 us; the launch traced here: 152 us
  waiting for transfers between devices  51.7 us (34%)
  starting transfers between devices  38.1 us (25%)
  blocking collectives  24.7 us (16%)
  Pallas kernels  19.1 us (12%)
  between operations  14.2 us (9%)
  other arithmetic  2.52 us (2%)
  local copies, waits for them, and re-layouts  1.89 us (1%)
    pallas_call x9, Pallas kernels, call(): pl.pallas_call(kernel, out_shape=shapes, in_specs=in_specs, out_specs=out...  19.1 us
    all_to_all x1, starting transfers between devices, on_device(): lax.all_to_all(pair.reshape(CHUNKS, PIECE, width), 'zl', 0, 0, tiled=True)  17.3 us
    all_to_all x1, waiting for transfers between devices, on_device(): mine = lax.all_to_all(copies, 'zl', 0, 0, tiled=True).reshape(HALF, width)  17.2 us
    all_to_all x1, waiting for transfers between devices, on_device(): lax.all_to_all(pair.reshape(CHUNKS, PIECE, width), 'zl', 0, 0, tiled=True)  16.7 us
    ppermute x2, waiting for transfers between devices, shift_rows(): return lax.ppermute(block, ('zh', 'x'), route)  13.6 us
    all_to_all x1, blocking collectives, on_device(): halo = lax.all_to_all(outgoing, 'y', 0, 0, tiled=True)  12.5 us
    all_to_all x1, blocking collectives, on_device(): back = lax.all_to_all(halo_back, 'y', 0, 0, tiled=True)  12.2 us
    ppermute x2, starting transfers between devices, shift_rows(): return lax.ppermute(block, ('zh', 'x'), route)  10.9 us
  transfers between devices with their start and end apart: 8, of which 6 were waited for; matrix products, arithmetic and copies ran while one was open for 2% of the time, Pallas kernels for 6%

profile of v5, /device:TPU:6, one launch (start us, length us, event | category | flops | bytes accessed | tf_op | source)
XLA Modules:
  0.0 152.2 jit_solution(3888781412950221625)
XLA Ops:
  7.2 1.8 %copies_kernel.1 = bf16[4,32,2688]{2,1,0:T(8,128)(2,1)} custom-call(bf16[32,2688]{1,0:T(8,128)(2,1)} %tokens_ref.1), custom_call_target="tpu_custom_call" | custom-call | bytes 860160 | tf_op jit(solution)/shard_map/copies_kernel/pallas_call | solution.py:263
  9.0 6.0 %all-to-all-start = ((bf16[4,32,2688]{2,1,0:T(8,128)(2,1)}), bf16[4,32,2688]{2,1,0:T(8,128)(2,1)S(1)}, u32[]{:S(2)}, u32[]{:S(2)}) async-start(bf16[4,32,2688]{2,1,0:T(8,128)(2,1)} %copies_kernel.1), calls=%async_computation | async-start | bytes 1376256 | tf_op jit(solution)/shard_map/all_to_all | solution.py:291
  15.8 17.2 %all-to-all-done = bf16[4,32,2688]{2,1,0:T(8,128)(2,1)S(1)} async-done(((bf16[4,32,2688]{2,1,0:T(8,128)(2,1)}), bf16[4,32,2688]{2,1,0:T(8,128)(2,1)S(1)}, u32[]{:S(2)}, u32[]{:S(2)}) %all-to-all-start) | async-done | bytes 688160 | tf_op jit(solution)/shard_map/all_to_all | solution.py:291
  33.0 1.9 %collective-permute-start = (bf16[128,2688]{1,0:T(8,128)(2,1)S(1)}, bf16[128,2688]{1,0:T(8,128)(2,1)S(1)}, u32[]{:S(2)}, u32[]{:S(2)}) collective-permute-start(bf16[128,2688]{1,0:T(8,128)(2,1)S(1)} %bitcast.7), channel_id=1, source_target_pairs={{0,1},{1,0},{2,3},{3,2},{4,5},{5,4},{6,7},{7,6},{8,9},{9,8},{10,11... | collective-permute-start | bytes 2064392 | tf_op jit(solution)/shard_map/ppermute | solution.py:32
  35.7 1.3 collective-permute-done.other
  37.1 2.1 %kv_kernel.1 = (bf16[256,256]{1,0:T(8,128)(2,1)S(1)}, f32[256,128]{1,0:T(8,128)}) custom-call(s32[3]{0:T(128)S(1)} %pad_add_fusion.place, bf16[128,2688]{1,0:T(8,128)(2,1)S(1)} %bitcast.8, bf16[128,2688]{1,0:T(8,128)(2,1)S(1)} %collective-permute-done.other, bf16[2688,128]{1,0:T(8,128)(2,1)S(1)} %copy-done, bf16[2688,128]{1,0:T(8,128)(2,1)S(1)} %copy-done.1, ...), custom_call_target="tpu_custom_call" | custom-call | bytes 3277324 | tf_op jit(solution)/shard_map/kv_kernel/pallas_call | solution.py:263
  39.2 9.0 %collective-permute-start.1 = (bf16[256,256]{1,0:T(8,128)(2,1)S(1)}, bf16[256,256]{1,0:T(8,128)(2,1)S(1)}, u32[]{:S(2)}, u32[]{:S(2)}) collective-permute-start(bf16[256,256]{1,0:T(8,128)(2,1)S(1)} %get-tuple-element.16.own), channel_id=1, source_target_pairs={{0,32},{32,64},{64,96},{96,128},{128,160},{160,192},{192,224},{224... | collective-permute-start | bytes 393224 | tf_op jit(solution)/shard_map/ppermute | solution.py:38
  48.2 2.0 %q_kernel.1 = (bf16[256,256]{1,0:T(8,128)(2,1)}, f32[256,256]{1,0:T(8,128)}) custom-call(s32[3]{0:T(128)S(1)} %pad_add_fusion.place, bf16[128,2688]{1,0:T(8,128)(2,1)S(1)} %bitcast.9, bf16[128,2688]{1,0:T(8,128)(2,1)S(1)} %collective-permute-done.other, bf16[2688,256]{1,0:T(8,128)(2,1)S(1)} %copy-done.2, f32[1,128]{1,0:T(1,128)S(1)} %bitcast.13, ...), custom_call_target="tpu_custom_call" | custom-call | bytes 3408396 | tf_op jit(solution)/shard_map/q_kernel/pallas_call | solution.py:263
  50.2 3.2 %collective-permute-done.1 = bf16[256,256]{1,0:T(8,128)(2,1)S(1)} collective-permute-done((bf16[256,256]{1,0:T(8,128)(2,1)S(1)}, bf16[256,256]{1,0:T(8,128)(2,1)S(1)}, u32[]{:S(2)}, u32[]{:S(2)}) %collective-permute-start.1) | collective-permute-done | bytes 131104 | tf_op jit(solution)/shard_map/ppermute | solution.py:38
  53.5 12.5 %all_to_all.20.halo = bf16[4,256,256]{2,1,0:T(8,128)(2,1)S(1)} all-to-all(bf16[4,256,256]{2,1,0:T(8,128)(2,1)S(1)} %broadcast_select_fusion), channel_id=1, replica_groups=mesh['zh'=4,'x'=4,'y'=4,'zl'=4,'c'=2] {'y'}, dimensions={0} | all-to-all | bytes 1048576 | tf_op jit(solution)/shard_map/all_to_all | solution.py:307
  66.1 7.4 %attention_kernel.1 = (bf16[256,2688]{1,0:T(8,128)(2,1)}, bf16[256,256]{1,0:T(8,128)(2,1)}, bf16[4,256,256]{2,1,0:T(8,128)(2,1)S(1)}, f32[256,256]{1,0:T(8,128)}) custom-call(s32[3]{0:T(128)S(1)} %pad_add_fusion.place, bf16[256,256]{1,0:T(8,128)(2,1)} %get-tuple-element.18.q, bf16[4,256,256]{2,1,0:T(8,128)(2,1)S(1)} %all_to_all.20.halo, ...), custom_call_target="tpu_custom_call" | custom-call | bytes 6357516 | tf_op jit(solution)/shard_map/attention_kernel/pallas_call | solution.py:263
  73.4 0.8 copy-done.8
  74.3 1.0 copy-done.9
  75.3 12.2 %all_to_all.21.back = bf16[4,256,256]{2,1,0:T(8,128)(2,1)S(1)} all-to-all(bf16[4,256,256]{2,1,0:T(8,128)(2,1)S(1)} %copy-done.9), channel_id=1, replica_groups=mesh['zh'=4,'x'=4,'y'=4,'zl'=4,'c'=2] {'y'}, dimensions={0} | all-to-all | bytes 1048576 | tf_op jit(solution)/shard_map/all_to_all | solution.py:328
  87.4 1.2 gather_kernel.1
  88.6 1.9 %collective-permute-start.2 = (bf16[256,256]{1,0:T(8,128)(2,1)S(1)}, bf16[256,256]{1,0:T(8,128)(2,1)S(1)}, u32[]{:S(2)}, u32[]{:S(2)}) collective-permute-start(bf16[256,256]{1,0:T(8,128)(2,1)S(1)} %get-tuple-element.28), channel_id=1, source_target_pairs={{32,0},{64,32},{96,64},{128,96},{160,128},{192,160},{224,192},{256... | collective-permute-start | bytes 393224 | tf_op jit(solution)/shard_map/ppermute | solution.py:38
  91.1 10.4 %collective-permute-done.2.below = bf16[256,256]{1,0:T(8,128)(2,1)S(1)} collective-permute-done((bf16[256,256]{1,0:T(8,128)(2,1)S(1)}, bf16[256,256]{1,0:T(8,128)(2,1)S(1)}, u32[]{:S(2)}, u32[]{:S(2)}) %collective-permute-start.2) | collective-permute-done | bytes 131104 | tf_op jit(solution)/shard_map/ppermute | solution.py:38
  101.6 1.2 end_given_kernel.1
  102.8 1.9 %collective-permute-start.3 = (bf16[128,2688]{1,0:T(8,128)(2,1)S(1)}, bf16[128,2688]{1,0:T(8,128)(2,1)S(1)}, u32[]{:S(2)}, u32[]{:S(2)}) collective-permute-start(bf16[128,2688]{1,0:T(8,128)(2,1)S(1)} %end_given_kernel.1), channel_id=1, source_target_pairs={{0,1},{1,0},{2,3},{3,2},{4,5},{5,4},{6,7},{7,6},{8,9},{9,8},{10,11... | collective-permute-start | bytes 2064392 | tf_op jit(solution)/shard_map/ppermute | solution.py:32
  104.8 2.1 %collective-permute-done.3.arrived = bf16[128,2688]{1,0:T(8,128)(2,1)S(1)} collective-permute-done((bf16[128,2688]{1,0:T(8,128)(2,1)S(1)}, bf16[128,2688]{1,0:T(8,128)(2,1)S(1)}, u32[]{:S(2)}, u32[]{:S(2)}) %collective-permute-start.3) | collective-permute-done | bytes 688160 | tf_op jit(solution)/shard_map/ppermute | solution.py:32
  106.9 2.1 %end_pair_kernel.1 = bf16[128,2688]{1,0:T(8,128)(2,1)} custom-call(s32[3]{0:T(128)S(1)} %pad_add_fusion.place, f32[256,2688]{1,0:T(8,128)S(1)} %base_kernel.1.base, f32[256,256]{1,0:T(8,128)S(1)} %get-tuple-element.27.own, bf16[256,256]{1,0:T(8,128)(2,1)S(1)} %collective-permute-done.2.below, f32[256,128]{1,0:T(8,128)S(1)} %copy-done.11, ...), custom_call_target="tpu_custom_call" | custom-call | bytes 6291980 | tf_op jit(solution)/shard_map/end_pair_kernel/pallas_call | solution.py:263
  109.0 17.3 %all-to-all-start.3 = ((bf16[4,32,2688]{2,1,0:T(8,128)(2,1)}), bf16[4,32,2688]{2,1,0:T(8,128)(2,1)S(1)}, u32[]{:S(2)}, u32[]{:S(2)}) async-start(bf16[4,32,2688]{2,1,0:T(8,128)(2,1)} %bitcast.6), calls=%async_computation.4 | async-start | bytes 1376256 | tf_op jit(solution)/shard_map/all_to_all | solution.py:339
  126.3 1.6 %add_convert_fusion = bf16[32,2688]{1,0:T(8,128)(2,1)} fusion(bf16[32,2688]{1,0:T(8,128)(2,1)} %reduce-scatter.2.cloned.1.call-done, bf16[32,2688]{1,0:T(8,128)(2,1)S(1)} %copy-done.15), kind=kLoop, calls=%fused_computation.1 | loop fusion | flops 344064 | bytes 516096 | tf_op jit(solution)/shard_map/convert_element_type | solution.py:340
  127.9 16.7 %all-to-all-done.3.pieces = bf16[4,32,2688]{2,1,0:T(8,128)(2,1)S(1)} async-done(((bf16[4,32,2688]{2,1,0:T(8,128)(2,1)}), bf16[4,32,2688]{2,1,0:T(8,128)(2,1)S(1)}, u32[]{:S(2)}, u32[]{:S(2)}) %all-to-all-start.3) | async-done | bytes 688160 | tf_op jit(solution)/shard_map/all_to_all | solution.py:339
  (45 shorter events, 3.1 us)
Async XLA Ops:
  9.0 28.1 %copy-start = (bf16[2688,128]{1,0:T(8,128)(2,1)S(1)}, bf16[2688,128]{1,0:T(8,128)(2,1)}, u32[]{:S(2)}) copy-start(bf16[2688,128]{1,0:T(8,128)(2,1)} %wk.5) | copy-start | bytes 2064388
  9.0 28.1 %copy-start.1 = (bf16[2688,128]{1,0:T(8,128)(2,1)S(1)}, bf16[2688,128]{1,0:T(8,128)(2,1)}, u32[]{:S(2)}) copy-start(bf16[2688,128]{1,0:T(8,128)(2,1)} %wv.5) | copy-start | bytes 2064388
  9.0 28.1 %copy-start.13 = (f32[128]{0:T(128)S(1)}, f32[128]{0:T(128)}, u32[]{:S(2)}) copy-start(f32[128]{0:T(128)} %param.15) | copy-start | bytes 1540
  9.0 24.0 %all-to-all-start = ((bf16[4,32,2688]{2,1,0:T(8,128)(2,1)}), bf16[4,32,2688]{2,1,0:T(8,128)(2,1)S(1)}, u32[]{:S(2)}, u32[]{:S(2)}) async-start(bf16[4,32,2688]{2,1,0:T(8,128)(2,1)} %copies_kernel.1), calls=%async_computation | async-start | bytes 1376256 | tf_op jit(solution)/shard_map/all_to_all | solution.py:291
  15.0 51.0 %all-gather.2.cloned.1.call-start = ((), (), s32[]{:S(2)}) async-start(), calls=%async_computation.5 | async-start | bytes 1548288 | tf_op jit(solution)/shard_map/all_gather | solution.py:288
  15.7 110.6 %reduce-scatter.2.cloned.1.call-start = ((), (), s32[]{:S(2)}) async-start(), calls=%async_computation.6 | async-start | bytes 1548288 | tf_op jit(solution)/shard_map/reduce_scatter | solution.py:327
  33.0 4.0 %collective-permute-start = (bf16[128,2688]{1,0:T(8,128)(2,1)S(1)}, bf16[128,2688]{1,0:T(8,128)(2,1)S(1)}, u32[]{:S(2)}, u32[]{:S(2)}) collective-permute-start(bf16[128,2688]{1,0:T(8,128)(2,1)S(1)} %bitcast.7), channel_id=1, source_target_pairs={{0,1},{1,0},{2,3},{3,2},{4,5},{5,4},{6,7},{7,6},{8,9},{9,8},{10,11... | collective-permute-start | bytes 2064392 | tf_op jit(solution)/shard_map/ppermute | solution.py:32
  35.7 12.5 %copy-start.3 = (f32[256,128]{1,0:T(8,128)}, f32[256,128]{1,0:T(8,128)S(1)}, u32[]{:S(2)}) copy-start(f32[256,128]{1,0:T(8,128)S(1)} %get-tuple-element.33.cos) | copy-start | bytes 393220
  35.7 12.5 %copy-start.5 = (f32[256,128]{1,0:T(8,128)}, f32[256,128]{1,0:T(8,128)S(1)}, u32[]{:S(2)}) copy-start(f32[256,128]{1,0:T(8,128)S(1)} %get-tuple-element.34.sin) | copy-start | bytes 393220
  37.1 11.1 %copy-start.2 = (bf16[2688,256]{1,0:T(8,128)(2,1)S(1)}, bf16[2688,256]{1,0:T(8,128)(2,1)}, u32[]{:S(2)}) copy-start(bf16[2688,256]{1,0:T(8,128)(2,1)} %wq.3) | copy-start | bytes 4128772
  37.1 11.1 %copy-start.14 = (f32[128]{0:T(128)S(1)}, f32[128]{0:T(128)}, u32[]{:S(2)}) copy-start(f32[128]{0:T(128)} %param.14) | copy-start | bytes 1540
  39.2 14.2 %copy-start.10 = (bf16[256,256]{1,0:T(8,128)(2,1)}, bf16[256,256]{1,0:T(8,128)(2,1)S(1)}, u32[]{:S(2)}) copy-start(bf16[256,256]{1,0:T(8,128)(2,1)S(1)} %get-tuple-element.16.own) | copy-start | bytes 393220
  39.2 14.2 %collective-permute-start.1 = (bf16[256,256]{1,0:T(8,128)(2,1)S(1)}, bf16[256,256]{1,0:T(8,128)(2,1)S(1)}, u32[]{:S(2)}, u32[]{:S(2)}) collective-permute-start(bf16[256,256]{1,0:T(8,128)(2,1)S(1)} %get-tuple-element.16.own), channel_id=1, source_target_pairs={{0,32},{32,64},{64,96},{96,128},{128,160},{160,192},{192,224},{224... | collective-permute-start | bytes 393224 | tf_op jit(solution)/shard_map/ppermute | solution.py:38
  73.4 0.8 copy-start.8
  74.2 1.0 copy-start.9
  74.2 16.3 %copy-start.12 = (bf16[256,256]{1,0:T(8,128)(2,1)S(1)}, bf16[256,256]{1,0:T(8,128)(2,1)}, u32[]{:S(2)}) copy-start(bf16[256,256]{1,0:T(8,128)(2,1)} %get-tuple-element.24.q_back) | copy-start | bytes 393220
  88.6 13.0 %collective-permute-start.2 = (bf16[256,256]{1,0:T(8,128)(2,1)S(1)}, bf16[256,256]{1,0:T(8,128)(2,1)S(1)}, u32[]{:S(2)}, u32[]{:S(2)}) collective-permute-start(bf16[256,256]{1,0:T(8,128)(2,1)S(1)} %get-tuple-element.28), channel_id=1, source_target_pairs={{32,0},{64,32},{96,64},{128,96},{160,128},{192,160},{224,192},{256... | collective-permute-start | bytes 393224 | tf_op jit(solution)/shard_map/ppermute | solution.py:38
  90.5 11.0 %copy-start.4 = (f32[256,128]{1,0:T(8,128)S(1)}, f32[256,128]{1,0:T(8,128)}, u32[]{:S(2)}) copy-start(f32[256,128]{1,0:T(8,128)} %copy-done.3) | copy-start | bytes 393220
  90.5 11.0 %copy-start.6 = (f32[256,128]{1,0:T(8,128)S(1)}, f32[256,128]{1,0:T(8,128)}, u32[]{:S(2)}) copy-start(f32[256,128]{1,0:T(8,128)} %copy-done.5) | copy-start | bytes 393220
  90.6 11.0 %copy-start.11 = (f32[256,128]{1,0:T(8,128)S(1)}, f32[256,128]{1,0:T(8,128)}, u32[]{:S(2)}) copy-start(f32[256,128]{1,0:T(8,128)} %get-tuple-element.29.k_raw) | copy-start | bytes 393220
  102.8 4.0 %collective-permute-start.3 = (bf16[128,2688]{1,0:T(8,128)(2,1)S(1)}, bf16[128,2688]{1,0:T(8,128)(2,1)S(1)}, u32[]{:S(2)}, u32[]{:S(2)}) collective-permute-start(bf16[128,2688]{1,0:T(8,128)(2,1)S(1)} %end_given_kernel.1), channel_id=1, source_target_pairs={{0,1},{1,0},{2,3},{3,2},{4,5},{5,4},{6,7},{7,6},{8,9},{9,8},{10,11... | collective-permute-start | bytes 2064392 | tf_op jit(solution)/shard_map/ppermute | solution.py:32
  109.0 17.3 %copy-start.15 = (bf16[32,2688]{1,0:T(8,128)(2,1)S(1)}, bf16[32,2688]{1,0:T(8,128)(2,1)}, u32[]{:S(2)}) copy-start(bf16[32,2688]{1,0:T(8,128)(2,1)} %tokens_ref.1) | copy-start | bytes 516100
  109.0 35.6 %copy-start.7 = (bf16[32,2688]{1,0:T(8,128)(2,1)S(1)}, bf16[32,2688]{1,0:T(8,128)(2,1)}, u32[]{:S(2)}) copy-start(bf16[32,2688]{1,0:T(8,128)(2,1)} %first.1) | copy-start | bytes 516100
  109.0 35.6 %all-to-all-start.3 = ((bf16[4,32,2688]{2,1,0:T(8,128)(2,1)}), bf16[4,32,2688]{2,1,0:T(8,128)(2,1)S(1)}, u32[]{:S(2)}, u32[]{:S(2)}) async-start(bf16[4,32,2688]{2,1,0:T(8,128)(2,1)} %bitcast.6), calls=%async_computation.4 | async-start | bytes 1376256 | tf_op jit(solution)/shard_map/all_to_all | solution.py:339
Sparse Core Ops, SparseCore 0:
  17.9 48.0 all-gather.1
  74.4 51.5 reduce-scatter.1
